TPU v7x, 128 devices: a whole 4x4x4 slice. The times are simulated.
128 devices in a mesh: mod: 2 (over x_hi), batch: 64 (over y, z, x_lo, core).
Axes of the slice: x: 4 (x_hi: 2, x_lo: 2; x = x_hi * 2 + x_lo), y: 4, z: 4, core: 2. Of those that a mesh axis runs over, the one named last changes fastest.
Arguments:
- hidden: bfloat16 [448, 2, 128, 768], P('batch', 'mod'), may hold values from -6 to 6
- text_counts: int32 [448], P('batch'), may hold values from 32 to 128, as said below
- region_counts: int32 [448], P('batch'), may hold values from 50 to 100, as said below
- qkv_weight: bfloat16 [1, 768, 2304], replicated, may hold values from -0.21875 to 0.21875
- qv_bias: bfloat16 [1, 1536], replicated, may hold values from -3 to 3
- out_weight: bfloat16 [1, 768, 768], replicated, may hold values from -1.75 to 1.75
- out_bias: bfloat16 [1, 768], replicated, may hold values from -2 to 2
- norm1_gain: bfloat16 [1, 768], replicated, may hold values from 0.5 to 1.5
- norm1_bias: bfloat16 [1, 768], replicated, may hold values from -2 to 2
- up_weight: bfloat16 [1, 768, 3072], replicated, may hold values from -0.21875 to 0.21875
- up_bias: bfloat16 [1, 3072], replicated, may hold values from -3 to 3
- down_weight: bfloat16 [1, 3072, 768], replicated, may hold values from -0.109375 to 0.109375
- down_bias: bfloat16 [1, 768], replicated, may hold values from -2 to 2
- norm2_gain: bfloat16 [1, 768], replicated, may hold values from 0.5 to 1.5
- norm2_bias: bfloat16 [1, 768], replicated, may hold values from -2 to 2
- out_grad: bfloat16 [448, 2, 128, 768], P('batch', 'mod'), may hold values from -6 to 6
Outputs:
- layer_out: bfloat16 [448, 2, 128, 768], P('batch', 'mod')
- input_grad: bfloat16 [448, 2, 128, 768], P('batch', 'mod')
- grad_qkv_weight: float32 [1, 768, 2304], replicated
- grad_qv_bias: float32 [1, 1536], replicated
- grad_out_weight: float32 [1, 768, 768], replicated
- grad_out_bias: float32 [1, 768], replicated
- grad_norm1_gain: float32 [1, 768], replicated
- grad_norm1_bias: float32 [1, 768], replicated
- grad_up_weight: float32 [1, 768, 3072], replicated
- grad_up_bias: float32 [1, 3072], replicated
- grad_down_weight: float32 [1, 3072, 768], replicated
- grad_down_bias: float32 [1, 768], replicated
- grad_norm2_gain: float32 [1, 768], replicated
- grad_norm2_bias: float32 [1, 768], replicated
Inputs may be any that keep to these rules, and one draw needn't show every extreme that they name: `text_counts`: valid caption tokens of each pair; they fill the first slots of its 128 text slots. `region_counts`: valid image regions of each pair; they fill the first slots of its 128 region slots.
All inputs are finite; a program needn't handle non-finite values.
Results may differ from a plain program's by a relative error of at most 0.014.
Values may be sent and summed in bfloat16 or wider, within the bound.
A program may use at most 256 MiB of HBM per device.

v0:
```python
from functools import partial

import jax
import jax.numpy as jnp
from jax import lax
from jax.sharding import PartitionSpec as P

HEADS = 12
HEAD_DIM = 64


norm_epsilon = 1e-06
masked_value = -1000000000.0


def partner(x, axis, distance):
    return lax.ppermute(x, axis, [(i, i ^ 1 << distance) for i in range(lax.axis_size(axis))])


def layer_norm(values, scaling, offset):
    centre = values - jnp.mean(values, -1, keepdims=True)
    spread = jnp.mean(centre * centre, -1, keepdims=True)
    return centre * lax.rsqrt(spread + norm_epsilon) * scaling + offset


def column_product(left, right):
    return lax.dot_general(
        left, right, (((0,), (0,)), ((), ())), preferred_element_type=jnp.float32
    )


def row_product(left, right):
    return lax.dot_general(
        left, right, (((1,), (1,)), ((), ())), preferred_element_type=jnp.float32
    )


def pair_scores(queries, key_rows, key_mask):
    raw_scores = jnp.einsum(
        "pqhe,pkhe->phqk", queries, key_rows, preferred_element_type=jnp.float32
    ) * HEAD_DIM ** (-0.5)
    return jnp.where(key_mask[:, None, None, :] > 0.5, raw_scores, masked_value)


def body(
    hidden,
    text_counts,
    region_counts,
    qkv_weight,
    qv_bias,
    out_weight,
    out_bias,
    norm1_gain,
    norm1_bias,
    up_weight,
    up_bias,
    down_weight,
    down_bias,
    norm2_gain,
    norm2_bias,
    out_grad,
):
    pair_count = hidden.shape[0]
    slot_count = hidden.shape[2]
    model_width = hidden.shape[3]
    depth_count = qkv_weight.shape[0]
    row_count = pair_count * slot_count
    head_shape = (pair_count, slot_count, HEADS, HEAD_DIM)
    score_scale = HEAD_DIM ** (-0.5)
    modality = lax.axis_index("mod")
    own_counts = jnp.where(modality == 0, text_counts, region_counts)
    other_counts = jnp.where(modality == 0, region_counts, text_counts)
    slot_index = jnp.arange(slot_count, dtype=jnp.int32)
    own_live = (slot_index[None, :] < own_counts[:, None]).astype(jnp.float32)
    other_live = (slot_index[None, :] < other_counts[:, None]).astype(jnp.float32)
    key_mask = jnp.concatenate([own_live, other_live], 1)
    row_mask = own_live.reshape(row_count, 1)
    current = hidden.reshape(row_count, model_width)
    depth = 0
    merged_bias = jnp.concatenate(
        [
            qv_bias[depth, :model_width].astype(jnp.float32),
            jnp.zeros((model_width,), jnp.float32),
            qv_bias[depth, model_width:].astype(jnp.float32),
        ]
    )
    merged = (
        jnp.dot(current, qkv_weight[depth], preferred_element_type=jnp.float32) + merged_bias
    ).astype(jnp.bfloat16)
    queries = merged[:, :model_width].reshape(head_shape)
    own_keys = merged[:, model_width : 2 * model_width]
    own_values = merged[:, 2 * model_width :]
    partner_keys, partner_values = partner((own_keys, own_values), "mod", 0)
    key_rows = jnp.concatenate([own_keys.reshape(head_shape), partner_keys.reshape(head_shape)], 1)
    value_rows = jnp.concatenate(
        [own_values.reshape(head_shape), partner_values.reshape(head_shape)], 1
    )
    scores = pair_scores(queries, key_rows, key_mask)
    highest = jnp.max(scores, -1, keepdims=True)
    log_total = highest + jnp.log(jnp.sum(jnp.exp(scores - highest), -1, keepdims=True))
    weights_low = jnp.exp(scores - log_total).astype(jnp.bfloat16)
    context = jnp.einsum(
        "phqk,pkhe->pqhe", weights_low, value_rows, preferred_element_type=jnp.float32
    )
    context = context.reshape(row_count, model_width).astype(jnp.bfloat16)
    attention = jnp.dot(context, out_weight[depth], preferred_element_type=jnp.float32) + out_bias[
        depth
    ].astype(jnp.float32)
    first_sum = current.astype(jnp.float32) + attention
    first_norm = layer_norm(
        first_sum, norm1_gain[depth].astype(jnp.float32), norm1_bias[depth].astype(jnp.float32)
    )
    first_low = first_norm.astype(jnp.bfloat16)
    pre_gelu = jnp.dot(first_low, up_weight[depth], preferred_element_type=jnp.float32) + up_bias[
        depth
    ].astype(jnp.float32)
    activated = jax.nn.gelu(pre_gelu, approximate=False).astype(jnp.bfloat16)
    second_sum = (
        first_norm
        + jnp.dot(activated, down_weight[depth], preferred_element_type=jnp.float32)
        + down_bias[depth].astype(jnp.float32)
    )
    layer_result = (
        layer_norm(
            second_sum, norm2_gain[depth].astype(jnp.float32), norm2_bias[depth].astype(jnp.float32)
        )
        * row_mask
    )
    kept_pair = None
    saved = [
        (
            current,
            merged,
            kept_pair,
            log_total,
            context,
            first_sum,
            first_low,
            pre_gelu,
            activated,
            second_sum,
        )
    ]
    current = layer_result.astype(jnp.bfloat16)
    layer_out = current.reshape(hidden.shape)
    upstream = out_grad.reshape(row_count, model_width).astype(jnp.float32)
    per_depth = [None] * depth_count
    for depth in reversed(range(depth_count)):
        (
            layer_input,
            merged,
            kept_pair,
            log_total,
            context,
            first_sum,
            first_low,
            pre_gelu,
            activated,
            second_sum,
        ) = saved[depth]
        masked_grad = upstream * row_mask
        second_value, second_pull = jax.vjp(
            layer_norm,
            second_sum,
            norm2_gain[depth].astype(jnp.float32),
            norm2_bias[depth].astype(jnp.float32),
        )
        second_grad, gain2_grad, bias2_grad = second_pull(masked_grad)
        branch_low = second_grad.astype(jnp.bfloat16)
        down_grad = column_product(activated, branch_low)
        down_bias_grad = jnp.sum(branch_low.astype(jnp.float32), 0)
        gelu_value, gelu_pull = jax.vjp(partial(jax.nn.gelu, approximate=False), pre_gelu)
        pre_grad = gelu_pull(row_product(branch_low, down_weight[depth]))[0].astype(jnp.bfloat16)
        up_grad = column_product(first_low, pre_grad)
        up_bias_grad = jnp.sum(pre_grad.astype(jnp.float32), 0)
        norm_grad = row_product(pre_grad, up_weight[depth]) + second_grad
        ffn_part = (up_grad, up_bias_grad, down_grad, down_bias_grad, gain2_grad, bias2_grad)
        first_value, first_pull = jax.vjp(
            layer_norm,
            first_sum,
            norm1_gain[depth].astype(jnp.float32),
            norm1_bias[depth].astype(jnp.float32),
        )
        sum_grad, gain1_grad, bias1_grad = first_pull(norm_grad)
        attention_low = sum_grad.astype(jnp.bfloat16)
        out_weight_grad = column_product(context, attention_low)
        out_bias_grad = jnp.sum(attention_low.astype(jnp.float32), 0)
        context_grad = (
            row_product(attention_low, out_weight[depth]).astype(jnp.bfloat16).reshape(head_shape)
        )
        queries = merged[:, :model_width].reshape(head_shape)
        own_keys = merged[:, model_width : 2 * model_width]
        own_values = merged[:, 2 * model_width :]
        partner_keys, partner_values = partner((own_keys, own_values), "mod", 0)
        key_rows = jnp.concatenate(
            [own_keys.reshape(head_shape), partner_keys.reshape(head_shape)], 1
        )
        value_rows = jnp.concatenate(
            [own_values.reshape(head_shape), partner_values.reshape(head_shape)], 1
        )
        scores = pair_scores(queries, key_rows, key_mask)
        weights_full = jnp.exp(scores - log_total)
        weights_low = weights_full.astype(jnp.bfloat16)
        weight_grad = jnp.einsum(
            "pqhe,pkhe->phqk", context_grad, value_rows, preferred_element_type=jnp.float32
        )
        value_grad = jnp.einsum(
            "phqk,pqhe->pkhe", weights_low, context_grad, preferred_element_type=jnp.float32
        )
        score_grad = weights_full * (
            weight_grad - jnp.sum(weights_full * weight_grad, -1, keepdims=True)
        )
        score_grad = score_grad.astype(jnp.bfloat16)
        query_grad = (
            jnp.einsum("phqk,pkhe->pqhe", score_grad, key_rows, preferred_element_type=jnp.float32)
            * score_scale
        )
        key_grad = (
            jnp.einsum("phqk,pqhe->pkhe", score_grad, queries, preferred_element_type=jnp.float32)
            * score_scale
        )
        back_keys, back_values = (
            partner(key_grad[:, slot_count:].astype(jnp.bfloat16), "mod", 0).astype(jnp.float32),
            partner(value_grad[:, slot_count:].astype(jnp.bfloat16), "mod", 0).astype(jnp.float32),
        )
        own_key_grad = (key_grad[:, :slot_count] + back_keys).reshape(row_count, model_width)
        own_value_grad = (value_grad[:, :slot_count] + back_values).reshape(row_count, model_width)
        merged_grad = jnp.concatenate(
            [query_grad.reshape(row_count, model_width), own_key_grad, own_value_grad], 1
        ).astype(jnp.bfloat16)
        merged_weight_grad = column_product(layer_input, merged_grad)
        merged_column = jnp.sum(merged_grad.astype(jnp.float32), 0)
        merged_bias_grad = jnp.concatenate(
            [merged_column[:model_width], merged_column[2 * model_width :]]
        )
        attention_part = (
            merged_weight_grad,
            merged_bias_grad,
            out_weight_grad,
            out_bias_grad,
            gain1_grad,
            bias1_grad,
        )
        per_depth[depth] = tuple(attention_part) + tuple(ffn_part)
        upstream = row_product(merged_grad, qkv_weight[depth]) + sum_grad
    input_grad = upstream.astype(jnp.bfloat16).reshape(hidden.shape)
    stacked = [jnp.stack([per_depth[0][member]]) for member in range(12)]
    stacked = lax.psum(
        (
            stacked[0],
            stacked[1],
            stacked[2],
            stacked[3],
            stacked[4],
            stacked[5],
            stacked[6],
            stacked[7],
            stacked[8],
            stacked[9],
            stacked[10],
            stacked[11],
        ),
        ("mod", "batch"),
    )
    return (
        layer_out,
        input_grad,
        stacked[0],
        stacked[1],
        stacked[2],
        stacked[3],
        stacked[4],
        stacked[5],
        stacked[6],
        stacked[7],
        stacked[8],
        stacked[9],
        stacked[10],
        stacked[11],
    )


def solution(mesh):
    return jax.shard_map(
        body,
        mesh=mesh,
        in_specs=(
            P("batch", "mod", None, None),
            P("batch"),
            P("batch"),
            P(),
            P(),
            P(),
            P(),
            P(),
            P(),
            P(),
            P(),
            P(),
            P(),
            P(),
            P(),
            P("batch", "mod", None, None),
        ),
        out_specs=(
            P("batch", "mod", None, None),
            P("batch", "mod", None, None),
            P(),
            P(),
            P(),
            P(),
            P(),
            P(),
            P(),
            P(),
            P(),
            P(),
            P(),
            P(),
        ),
        check_vma=False,
    )
```

profile of v0, /device:TPU:1, one launch (start us, length us, event | category | flops | bytes accessed | tf_op | source)
XLA Modules:
  0.0 572.7 jit_solution(282655607934150982)
XLA Ops:
  9.2 5.3 add_convert_fusion.1
  16.6 3.6 collective-permute-start.1
  29.3 4.0 reshape.215
  33.4 4.0 reshape.216
  37.4 4.0 reshape.213
  52.4 4.0 reshape.217
  56.4 23.0 %collective-permute-done = bf16[896,768]{1,0:T(8,128)(2,1)} collective-permute-done((bf16[896,768]{1,0:T(8,128)(2,1)}, bf16[896,768]{1,0:T(8,128)(2,1)}, u32[]{:S(2)}, u32[]{:S(2)}) %collective-permute-start) | collective-permute-done | bytes 1376288 | tf_op jit(solution)/shard_map/ppermute | solution.py:17
  81.9 4.0 reshape.214
  89.0 4.8 fusion.6
  93.8 4.1 exponential_reduce_fusion
  99.9 3.6 fusion.32
  108.2 31.3 %multiply_convert_fusion.1 = (bf16[896,3072]{1,0:T(8,128)(2,1)S(1)}, f32[896,3072]{1,0:T(8,128)}, f32[896,3072]{1,0:T(8,128)}) fusion(f32[3072]{0:T(1024)S(1)} %bitcast.147, bf16[1,768,3072]{2,1,0:T(8,128)(2,1)S(1)} %bitcast.153, f32[896,768]{1,0:T(8,128)S(1)} %get-tuple-element.84, f32[768]{0:T(1024)S(1)} %get-tuple-element.93, ...), kind=kOutput, calls=%fused_computation.6 | convolution fusion | flops 4412964864 | bytes 35021824 | tf_op jit(solution)/shard_map/dot_general | solution.py:114
  139.5 4.7 fusion.64
  150.1 16.0 %convert_reduce_fusion = (f32[3072]{0:T(1024)}, bf16[896,3072]{1,0:T(8,128)(2,1)}) fusion(f32[896,3072]{1,0:T(8,128)} %get-tuple-element.70, bf16[896,768]{1,0:T(8,128)(2,1)S(1)} %get-tuple-element.62, bf16[1,3072,768]{2,1,0:T(8,128)(2,1)} %param.27, f32[896,3072]{1,0:T(8,128)} %get-tuple-element.85, f32[3072]{0:T(1024)S(1)} %bitcast.148), kind=kOutput, calls=%fused_computation.2 | convolution fusion | flops 4274648064 | bytes 33644544 | tf_op jit(solution)/shard_map/dot_general | solution.py:33
  166.1 9.8 %multiply_reduce_fusion.3 = (f32[768]{0:T(1024)}, f32[896]{0:T(1024)S(1)}, f32[768]{0:T(1024)}, f32[896,768]{1,0:T(8,128)S(1)}) fusion(f32[896,768]{1,0:T(8,128)S(1)} %get-tuple-element.84, f32[896]{0:T(1024)S(1)} %fusion.49, f32[896]{0:T(1024)S(1)} %broadcast_multiply_fusion.1, f32[768]{0:T(1024)S(1)} %get-tuple-element.94, ...), kind=kOutput, calls=%fused_computation.54 | convolution fusion | flops 4234737408 | bytes 18504704 | tf_op jit(solution)/shard_map/dot_general | solution.py:33
  175.9 8.2 %convolution_bitcast_fusion.1 = f32[1,768,3072]{2,1,0:T(8,128)} fusion(bf16[896,3072]{1,0:T(8,128)(2,1)S(1)} %copy-done.7, f32[896,768]{1,0:T(8,128)S(1)} %get-tuple-element.84, f32[768]{0:T(1024)S(1)} %get-tuple-element.93, f32[768]{0:T(1024)S(1)} %get-tuple-element.94, f32[896]{0:T(1024)S(1)} %fusion.49, f32[896]{0:T(1024)S(1)} %broadcast_multiply_fusion.1), kind=kOutput, calls=%fused_computation.28 | convolution fusion | flops 4231299072 | bytes 17708032 | tf_op jit(solution)/shard_map/dot_general | solution.py:27
  192.9 4.0 reshape.219
  196.9 6.2 %convolution_bitcast_fusion.3 = f32[7,256,12,64]{1,3,2,0:T(8,128)S(1)} fusion(bf16[7,128,12,64]{1,0,3,2:T(8,128)(2,1)} %reshape.219, f32[7,12,128,256]{3,2,1,0:T(8,128)} %copy-done.1, f32[7,12,128]{2,1,0:T(8,128)} %copy-done.19, pred[7,256]{1,0:T(8,128)(4,1)S(1)} %maximum_compare_fusion), kind=kOutput, calls=%fused_computation.70 | convolution fusion | flops 363331584 | bytes 17936128 | tf_op jit(solution)/shard_map/phqk,pqhe->pkhe/dot_general | solution.py:207
  203.1 10.6 %multiply_reduce_fusion = (f32[7,12,128]{2,1,0:T(8,128)S(1)}, f32[7,12,128,256]{3,2,1,0:T(8,128)}) fusion(f32[7,12,128,256]{3,2,1,0:T(8,128)} %copy-done.1, f32[7,12,128]{2,1,0:T(8,128)S(1)} %copy-done.20, pred[7,256]{1,0:T(8,128)(4,1)S(1)} %maximum_compare_fusion, bf16[7,256,12,64]{1,3,2,0:T(8,128)(2,1)} %copy-done.12, ...), kind=kOutput, calls=%fused_computation.4 | convolution fusion | flops 366073344 | bytes 26236672 | tf_op jit(solution)/shard_map/pqhe,pkhe->phqk/dot_general | solution.py:204
  213.7 7.8 %multiply_convert_fusion = bf16[7,12,128,256]{3,2,1,0:T(8,128)(2,1)S(1)} fusion(f32[7,12,128,256]{3,2,1,0:T(8,128)} %get-tuple-element.90, f32[7,12,128,256]{3,2,1,0:T(8,128)S(1)} %bitcast.138, f32[7,12,128]{2,1,0:T(8,128)S(1)} %get-tuple-element.89, f32[7,12,128]{2,1,0:T(8,128)S(1)} %copy-done.20, pred[7,256]{1,0:T(8,128)(4,1)S(1)} %maximum_compare_fusion), kind=kLoop, calls=%fused_computation.3 | loop fusion | flops 16515072 | bytes 27612928 | tf_op jit(solution)/shard_map/convert_element_type | solution.py:213
  221.6 3.9 fusion.31
  235.2 7.9 %convolution_bitcast_fusion = f32[1,3072,768]{2,1,0:T(8,128)} fusion(bf16[896,3072]{1,0:T(8,128)(2,1)S(1)} %bitcast.159, bf16[896,768]{1,0:T(8,128)(2,1)S(1)} %copy-done.16), kind=kOutput, calls=%fused_computation.27 | convolution fusion | flops 4227858432 | bytes 16318464 | tf_op jit(solution)/shard_map/dot_general | solution.py:27
  243.1 15.6 %collective-permute-done.3 = bf16[7,128,12,64]{1,3,2,0:T(8,128)(2,1)S(1)} collective-permute-done((bf16[7,128,12,64]{1,3,2,0:T(8,128)(2,1)S(1)}, bf16[7,128,12,64]{1,3,2,0:T(8,128)(2,1)S(1)}, u32[]{:S(2)}, u32[]{:S(2)}) %collective-permute-start.3) | collective-permute-done | bytes 1376288 | tf_op jit(solution)/shard_map/ppermute | solution.py:17
  260.2 27.9 %collective-permute-done.2 = bf16[7,128,12,64]{1,3,2,0:T(8,128)(2,1)S(1)} collective-permute-done((bf16[7,128,12,64]{1,3,2,0:T(8,128)(2,1)S(1)}, bf16[7,128,12,64]{1,3,2,0:T(8,128)(2,1)S(1)}, u32[]{:S(2)}, u32[]{:S(2)}) %collective-permute-start.2) | collective-permute-done | bytes 1376288 | tf_op jit(solution)/shard_map/ppermute | solution.py:17
  292.5 5.8 %convolution_bitcast_fusion.2 = f32[1,768,2304]{1,2,0:T(8,128)} fusion(bf16[896,2304]{0,1:T(8,128)(2,1)S(1)} %bitcast_dynamic-update-slice_fusion, bf16[896,768]{1,0:T(8,128)(2,1)S(1)} %bitcast.156), kind=kOutput, calls=%fused_computation.29 | convolution fusion | flops 3170893824 | bytes 12582912 | tf_op jit(solution)/shard_map/dot_general | solution.py:27
  308.3 70.7 %all-reduce = (f32[1,1536]{1,0:T(1,128)}, f32[1,768]{1,0:T(1,128)}, f32[1,768]{1,0:T(1,128)}, f32[1,768]{1,0:T(1,128)}, f32[1,3072]{1,0:T(1,128)}, /*index=5*/f3...) all-reduce(f32[1,1536]{1,0:T(1,128)S(1)} %stack.29, ...), channel_id=1, replica_groups=mesh['mod'=2,'batch'=64] {'mod','batch'}, use_global_device_ids=true, to_apply=%region_13.14 | all-reduce | flops 9216 | bytes 73728 | tf_op jit(solution)/shard_map/psum | solution.py:248
  379.0 8.0 %add_convert_fusion.2 = bf16[896,768]{1,0:T(8,128)(2,1)} fusion(f32[896,768]{1,0:T(8,128)} %copy-done.6, bf16[896,2304]{0,1:T(8,128)(2,1)} %copy-done.8, bf16[1,768,2304]{2,1,0:T(8,128)(2,1)S(1)} %copy-done, f32[896]{0:T(1024)S(1)} %copy-done.27), kind=kOutput, calls=%fused_computation.56 | convolution fusion | flops 3172958208 | bytes 11800064 | tf_op jit(solution)/shard_map/dot_general | solution.py:33
  387.0 154.5 %all-reduce.4.cloned.1.call-done = (f32[1,768,2304]{1,2,0:T(8,128)}, f32[1,768,768]{2,1,0:T(8,128)}, f32[1,768,3072]{2,1,0:T(8,128)}, f32[1,3072,768]{2,1,0:T(8,128)}) async-done(((f32[1,768,2304]{1,2,0:T(8,128)}, f32[1,768,768]{2,1,0:T(8,128)}, f32[1,768,3072]{2,1,0:T(8,128)}, f32[1,3072,768]{2,1,0:T(8,128)}), (f32[1,768,2304]{1,2,0:T(8,128)}, f32[1,768,768]{2,1,0:T(8,128)}, f32[1,768,3072]{2,1,0:T(8,128)}, ...) | async-done | bytes 28311568 | tf_op jit(solution)/shard_map/psum | solution.py:248
  541.5 8.0 %copy.61 = f32[1,768,2304]{2,1,0:T(8,128)} copy(f32[1,768,2304]{1,2,0:T(8,128)} %get-tuple-element.57) | data formatting | bytes 14155776
  549.4 3.4 copy.103
  552.8 8.8 %copy.104 = f32[1,768,3072]{2,1,0:T(8,128)} copy(f32[1,768,3072]{2,1,0:T(8,128)} %get-tuple-element.105) | data formatting | bytes 18874368
  561.6 3.7 copy.105
  (180 shorter events, 76.3 us)
Async XLA Ops:
  7.2 534.3 %all-reduce.4.cloned.1.call-start = ((), (), s32[]{:S(2)}) async-start(), calls=%async_computation | async-start | bytes 56623104 | tf_op jit(solution)/shard_map/psum | solution.py:248
  14.5 5.9 %copy-start.34 = (s32[7]{0:T(128)S(1)}, s32[7]{0:T(128)}, u32[]{:S(2)}) copy-start(s32[7]{0:T(128)} %param.17) | copy-start | bytes 88
  14.5 5.9 %copy-start.35 = (s32[7]{0:T(128)S(1)}, s32[7]{0:T(128)}, u32[]{:S(2)}) copy-start(s32[7]{0:T(128)} %param.18) | copy-start | bytes 88
  16.6 33.3 %collective-permute-start.1 = (bf16[896,768]{1,0:T(8,128)(2,1)}, bf16[896,768]{1,0:T(8,128)(2,1)}, u32[]{:S(2)}, u32[]{:S(2)}) collective-permute-start(bf16[896,768]{1,0:T(8,128)(2,1)} %get-tuple-element.72), channel_id=1, source_target_pairs={{0,64},{64,0},{1,65},{65,1},{2,66},{66,2},{3,67},{67,3},{4,68},{68... | collective-permute-start | bytes 4128776 | tf_op jit(solution)/shard_map/ppermute | solution.py:17
  20.2 59.2 %collective-permute-start = (bf16[896,768]{1,0:T(8,128)(2,1)}, bf16[896,768]{1,0:T(8,128)(2,1)}, u32[]{:S(2)}, u32[]{:S(2)}) collective-permute-start(bf16[896,768]{1,0:T(8,128)(2,1)} %get-tuple-element.73), channel_id=1, source_target_pairs={{0,64},{64,0},{1,65},{65,1},{2,66},{66,2},{3,67},{67,3},{4,68},{68... | collective-permute-start | bytes 4128776 | tf_op jit(solution)/shard_map/ppermute | solution.py:17
  33.4 8.7 %copy-start.32 = (bf16[1,768]{1,0:T(2,128)(2,1)S(1)}, bf16[1,768]{1,0:T(2,128)(2,1)}, u32[]{:S(2)}) copy-start(bf16[1,768]{1,0:T(2,128)(2,1)} %param.22) | copy-start | bytes 4612
  33.4 9.3 %copy-start.33 = (bf16[1,768]{1,0:T(2,128)(2,1)S(1)}, bf16[1,768]{1,0:T(2,128)(2,1)}, u32[]{:S(2)}) copy-start(bf16[1,768]{1,0:T(2,128)(2,1)} %param.28) | copy-start | bytes 4612
  41.4 6.9 %copy-start.9 = (bf16[7,128,12,64]{1,0,3,2:T(8,128)(2,1)S(1)}, bf16[7,128,12,64]{1,0,3,2:T(8,128)(2,1)}, u32[]{:S(2)}) copy-start(bf16[7,128,12,64]{1,0,3,2:T(8,128)(2,1)} %reshape.213) | copy-start | bytes 4128772
  93.8 6.1 %copy-start.1 = (f32[7,12,128,256]{3,2,1,0:T(8,128)}, f32[7,12,128,256]{3,2,1,0:T(8,128)S(1)}, u32[]{:S(2)}) copy-start(f32[7,12,128,256]{3,2,1,0:T(8,128)S(1)} %get-tuple-element.82) | copy-start | bytes 33030148
  93.8 5.5 copy-start.11
  105.2 34.3 %slice-start.6 = ((s8[4718592]{0:T(1024)(128)(4,1)}), s8[4194304]{0:T(1024)(128)(4,1)S(1)}, s32[]{:S(2)}) async-start(s8[4718592]{0:T(1024)(128)(4,1)} %bitcast.150), calls=%async_computation.7 | async-start | bytes 8388608
  108.2 31.3 %copy-start.30 = (f32[768]{0:T(1024)S(1)}, f32[768]{0:T(1024)}, u32[]{:S(2)}) copy-start(f32[768]{0:T(1024)} %convert_reduce_fusion.6) | copy-start | bytes 9220
  108.2 31.3 %slice-start.7 = ((s8[4718592]{0:T(1024)(128)(4,1)}), s8[524288]{0:T(1024)(128)(4,1)S(1)}, s32[]{:S(2)}) async-start(s8[4718592]{0:T(1024)(128)(4,1)} %bitcast.150), calls=%async_computation.8 | async-start | bytes 1048576
  139.4 4.8 copy-start.39
  150.1 16.0 %copy-start.15 = (bf16[896,768]{1,0:T(8,128)(2,1)}, bf16[896,768]{1,0:T(8,128)(2,1)S(1)}, u32[]{:S(2)}) copy-start(bf16[896,768]{1,0:T(8,128)(2,1)S(1)} %get-tuple-element.62) | copy-start | bytes 4128772
  166.1 9.8 %copy-start.7 = (bf16[896,3072]{1,0:T(8,128)(2,1)S(1)}, bf16[896,3072]{1,0:T(8,128)(2,1)}, u32[]{:S(2)}) copy-start(bf16[896,3072]{1,0:T(8,128)(2,1)} %get-tuple-element.92) | copy-start | bytes 16515076
  185.1 5.3 copy-start.26
  196.9 6.2 %copy-start.2 = (bf16[7,128,12,64]{1,0,3,2:T(8,128)(2,1)S(1)}, bf16[7,128,12,64]{1,0,3,2:T(8,128)(2,1)}, u32[]{:S(2)}) copy-start(bf16[7,128,12,64]{1,0,3,2:T(8,128)(2,1)} %reshape.219) | copy-start | bytes 4128772
  196.9 6.2 %copy-start.20 = (f32[7,12,128]{2,1,0:T(8,128)S(1)}, f32[7,12,128]{2,1,0:T(8,128)}, u32[]{:S(2)}) copy-start(f32[7,12,128]{2,1,0:T(8,128)} %copy-done.19) | copy-start | bytes 129028
  196.9 16.8 %slice-start = ((s8[11010048]{0:T(1024)(128)(4,1)}), s8[4194304]{0:T(1024)(128)(4,1)S(1)}, s32[]{:S(2)}) async-start(s8[11010048]{0:T(1024)(128)(4,1)} %bitcast.137), calls=%async_computation.1 | async-start | bytes 8388608
  196.9 16.8 %slice-start.1 = ((s8[11010048]{0:T(1024)(128)(4,1)}), s8[4194304]{0:T(1024)(128)(4,1)S(1)}, s32[]{:S(2)}) async-start(s8[11010048]{0:T(1024)(128)(4,1)} %bitcast.137), calls=%async_computation.2 | async-start | bytes 8388608
  203.1 10.6 %slice-start.2 = ((s8[11010048]{0:T(1024)(128)(4,1)}), s8[2621440]{0:T(1024)(128)(4,1)S(1)}, s32[]{:S(2)}) async-start(s8[11010048]{0:T(1024)(128)(4,1)} %bitcast.137), calls=%async_computation.3 | async-start | bytes 5242880
  225.5 4.5 copy-start.14
  225.5 4.5 copy-start.18
  225.5 9.4 %slice-start.10 = ((s8[5505024]{0:T(1024)(128)(4,1)}), s8[4194304]{0:T(1024)(128)(4,1)S(1)}, s32[]{:S(2)}) async-start(s8[5505024]{0:T(1024)(128)(4,1)} %bitcast.158), calls=%async_computation.11 | async-start | bytes 8388608
  226.8 8.2 %slice-start.11 = ((s8[5505024]{0:T(1024)(128)(4,1)}), s8[1310720]{0:T(1024)(128)(4,1)S(1)}, s32[]{:S(2)}) async-start(s8[5505024]{0:T(1024)(128)(4,1)} %bitcast.158), calls=%async_computation.12 | async-start | bytes 2621440
  226.8 31.9 %collective-permute-start.3 = (bf16[7,128,12,64]{1,3,2,0:T(8,128)(2,1)S(1)}, bf16[7,128,12,64]{1,3,2,0:T(8,128)(2,1)S(1)}, u32[]{:S(2)}, u32[]{:S(2)}) collective-permute-start(bf16[7,128,12,64]{1,3,2,0:T(8,128)(2,1)S(1)} %slice.68), channel_id=1, source_target_pairs={{0,64},{64,0},{1,65},{65,1},{2,66},{66,2},{3,67},{67,3},{4,68},{68... | collective-permute-start | bytes 4128776 | tf_op jit(solution)/shard_map/ppermute | solution.py:17
  234.1 54.0 %collective-permute-start.2 = (bf16[7,128,12,64]{1,3,2,0:T(8,128)(2,1)S(1)}, bf16[7,128,12,64]{1,3,2,0:T(8,128)(2,1)S(1)}, u32[]{:S(2)}, u32[]{:S(2)}) collective-permute-start(bf16[7,128,12,64]{1,3,2,0:T(8,128)(2,1)S(1)} %slice.69), channel_id=1, source_target_pairs={{0,64},{64,0},{1,65},{65,1},{2,66},{66,2},{3,67},{67,3},{4,68},{68... | collective-permute-start | bytes 4128776 | tf_op jit(solution)/shard_map/ppermute | solution.py:17
  302.4 76.6 %copy-start.27 = (f32[896]{0:T(1024)S(1)}, f32[896]{0:T(1024)}, u32[]{:S(2)}) copy-start(f32[896]{0:T(1024)} %copy-done.26) | copy-start | bytes 10756
  549.4 12.1 %slice-start.3 = ((s8[9437184]{0:T(1024)(128)(4,1)}), s8[4194304]{0:T(1024)(128)(4,1)S(1)}, s32[]{:S(2)}) async-start(s8[9437184]{0:T(1024)(128)(4,1)} %bitcast.139), calls=%async_computation.4 | async-start | bytes 8388608
  552.8 8.8 %slice-start.4 = ((s8[9437184]{0:T(1024)(128)(4,1)}), s8[4194304]{0:T(1024)(128)(4,1)S(1)}, s32[]{:S(2)}) async-start(s8[9437184]{0:T(1024)(128)(4,1)} %bitcast.139), calls=%async_computation.5 | async-start | bytes 8388608
  552.8 8.8 %slice-start.5 = ((s8[9437184]{0:T(1024)(128)(4,1)}), s8[1048576]{0:T(1024)(128)(4,1)S(1)}, s32[]{:S(2)}) async-start(s8[9437184]{0:T(1024)(128)(4,1)} %bitcast.139), calls=%async_computation.6 | async-start | bytes 2097152
  (25 other events, 55.1 us)
Sparse Core Ops, SparseCore 0:
  298.4 242.9 all-reduce.3
where the time goes:
time: 576 us; the launch traced here: 573 us
  waiting for transfers between devices  221 us (38%)
  matrix products  134 us (23%)
  local copies, waits for them, and re-layouts  94.2 us (16%)
  blocking collectives  70.7 us (12%)
  other arithmetic  30.2 us (5%)
  between operations  15.3 us (3%)
  starting transfers between devices  7.56 us (1%)
    psum x1, waiting for transfers between devices, body(): lax.psum((stacked[0], stacked[1], stacked[2], stacked[3], stacked[4], sta...  154 us
    psum x1, blocking collectives, body(): lax.psum((stacked[0], stacked[1], stacked[2], stacked[3], stacked[4], sta...  70.7 us
    ppermute x4, waiting for transfers between devices, partner(): lax.ppermute(x, axis, [(i, i ^ 1 << distance) for i in range(lax.axis_siz...  66.7 us
    unnamed x112, local copies, waits for them, and re-layouts  39.3 us
    dot_general x4, matrix products, row_product(): lax.dot_general(left, right, (((1,), (1,)), ((), ())), preferred_element_...  36.2 us
    dot_general x1, matrix products, body(): jnp.dot(first_low, up_weight[depth], preferred_element_type=jnp.float32)  31.3 us
    dot_general x4, matrix products, column_product(): lax.dot_general(left, right, (((0,), (0,)), ((), ())), preferred_element_...  24.7 us
  transfers between devices with their start and end apart: 5, of which 5 were waited for; matrix products, arithmetic and copies ran while one was open for 12% of the time, Pallas kernels for 0%

commit v1 on v0

--- a/solution.py
+++ b/solution.py
@@ -1,9 +1,153 @@
+import functools
 from functools import partial
 
 import jax
 import jax.numpy as jnp
 from jax import lax
+from jax.experimental import pallas as pl
+from jax.experimental.pallas import tpu as pltpu
 from jax.sharding import PartitionSpec as P
+
+MESH = pl.DeviceIdType.MESH
+LANES = 128
+
+def place():
+    mod, batch = lax.axis_index("mod"), lax.axis_index("batch")
+    return mod * 2 + lax.rem(batch // 2, 2), batch // 16, lax.rem(batch // 4, 4), lax.rem(batch, 2)
+
+def device(x, y, z, core):
+    return (x // 2, y * 16 + z * 4 + lax.rem(x, 2) * 2 + core)
+
+def near(v):
+    return v + 1 - 2 * lax.rem(v, 2)
+
+def neighbours():
+    x, y, z, core = place()
+    targets = [device(near(x), y, z, core), device(x, near(y), z, core), device(x, y, near(z), core),
+               device(3 - x, y, z, core), device(x, 3 - y, z, core), device(x, y, 3 - z, core)]
+    bits = [lax.rem((v + 1) // 2, 2) for v in (x, y, z)] + [v // 2 for v in (x, y, z)]
+    return targets, bits, device(x, y, z, 1 - core), core
+
+class Stream:
+    def __init__(self, blocks, rows):
+        self.blocks, self.rows = blocks, rows
+        self.half = blocks // 2
+        self.part = self.half // 6
+        assert self.part % 2 == 0
+        self.shapes = []
+        r, b = rows, self.part
+        for s in range(4):
+            r //= 2
+            self.shapes.append((b, r))
+        b //= 2
+        self.shapes.append((b, r))
+        self.shapes.append((b, r))
+
+    def scratch(self):
+        return [pltpu.VMEM((self.half, self.rows, LANES), jnp.bfloat16),
+                pltpu.VMEM((self.half, self.rows, LANES), jnp.bfloat16)] + [
+                pltpu.VMEM((6, b, r, LANES), jnp.bfloat16) for b, r in self.shapes] + [
+                pltpu.SemaphoreType.DMA((6, 8)), pltpu.SemaphoreType.DMA((6, 8)),
+                pltpu.SemaphoreType.DMA((6, 6)), pltpu.SemaphoreType.DMA((6, 6))]
+
+def ar_kernel(stream, g_ref, o_ref, acc, corebuf, r0, r1, r2, r3, r4, r5, ssem, rsem, sag, rag):
+    S = stream
+    recv = [r0, r1, r2, r3, r4, r5]
+    targets, bits, sibling, core = neighbours()
+    bar = pltpu.get_barrier_semaphore()
+    for t in targets + [sibling]:
+        pl.semaphore_signal(bar, inc=1, device_id=t, device_id_type=MESH)
+    pl.semaphore_wait(bar, 7)
+    width = S.part
+    def remote(src, dst, a, b, t):
+        return pltpu.make_async_remote_copy(src, dst, a, b, device_id=t, device_id_type=MESH)
+    cc, lc = [], []
+    for p in range(6):
+        c = remote(g_ref.at[pl.ds((1 - core) * S.half + p * width, width)], corebuf.at[pl.ds(p * width, width)], ssem.at[p, 0], rsem.at[p, 0], sibling)
+        c.start(); cc.append(c)
+        l = pltpu.make_async_copy(g_ref.at[pl.ds(core * S.half + p * width, width)], acc.at[pl.ds(p * width, width)], ssem.at[p, 7])
+        l.start(); lc.append(l)
+    reg = [[p * width, 0] for p in range(6)]
+    cur = (width, S.rows)
+    def add(dst, src, b, rows, chunk=48):
+        n = rows // chunk
+        def body(i, _):
+            k, r = i // n, lax.rem(i, n) * chunk
+            dst(k, r, chunk)[...] = dst(k, r, chunk)[...] + src(k, r, chunk)[...]
+            return 0
+        lax.fori_loop(0, b * n, body, 0)
+    pending = {}
+    def begin(p, s):
+        b, r = S.shapes[s]
+        d = (p + s) % 6
+        bit = bits[d]
+        bo, ro = reg[p]
+        if s < 4:
+            src = acc.at[pl.ds(bo, b), pl.ds(pl.multiple_of(ro + (1 - bit) * r, 16), r)]
+            reg[p] = [bo, ro + bit * r]
+        elif s == 4:
+            src = acc.at[pl.ds(bo + (1 - bit) * b, b), pl.ds(pl.multiple_of(ro, 16), r)]
+            reg[p] = [bo + bit * b, ro]
+        else:
+            src = acc.at[pl.ds(bo, b), pl.ds(pl.multiple_of(ro, 16), r)]
+        c = remote(src, recv[s].at[p], ssem.at[p, s + 1], rsem.at[p, s + 1], targets[d])
+        c.start()
+        pending[p, s] = c
+    def finish(p, s):
+        b, r = S.shapes[s]
+        bo, ro = reg[p]
+        c = pending.pop((p, s))
+        if s == 5: c.wait()
+        else:
+            c.wait_recv()
+            c.wait_send()
+        ch = 48
+        add(lambda k, rr, n: acc.at[bo + k, pl.ds(pl.multiple_of(ro + rr, 16), n)], lambda k, rr, n: recv[s].at[p, k, pl.ds(pl.multiple_of(rr, 16), n)], b, r, ch)
+    for p in range(6):
+        cc[p].wait(); lc[p].wait()
+        add(lambda k, rr, n: acc.at[p * width + k, pl.ds(pl.multiple_of(rr, 16), n)], lambda k, rr, n: corebuf.at[p * width + k, pl.ds(pl.multiple_of(rr, 16), n)], width, S.rows, 192)
+        begin(p, 0)
+    for s in range(6):
+        for p in range(6):
+            finish(p, s)
+            if s < 5: begin(p, s + 1)
+            else:
+                b, r = S.shapes[5]
+                bo, ro = reg[p]
+                l = pltpu.make_async_copy(acc.at[pl.ds(bo, b), pl.ds(pl.multiple_of(ro, 16), r)],
+                                          o_ref.at[pl.ds(core * S.half + bo, b), pl.ds(pl.multiple_of(ro, 16), r)], sag.at[p, 5])
+                l.start(); pending[p, "l"] = l
+    def gather(p, s):
+        b, r = S.shapes[s]
+        bo, ro = reg[p]
+        d = (p + s) % 6
+        ref = o_ref.at[pl.ds(core * S.half + bo, b), pl.ds(pl.multiple_of(ro, 16), r)]
+        c = remote(ref, ref, sag.at[p, s], rag.at[p, s], targets[d])
+        c.start(); pending[p, s] = c
+        bit = bits[d]
+        if s == 4: reg[p] = [bo - bit * b, ro]
+        else: reg[p] = [bo, ro - bit * r]
+    for p in range(6):
+        pending.pop((p, "l")).wait()
+        gather(p, 4)
+    for s in range(4, -1, -1):
+        for p in range(6):
+            pending.pop((p, s)).wait()
+            if s > 0: gather(p, s - 1)
+            else:
+                ref = o_ref.at[pl.ds(core * S.half + p * width, width)]
+                c = remote(ref, ref, ssem.at[p, 7], rag.at[p, 5], sibling)
+                c.start(); pending[p, "c"] = c
+    for p in range(6):
+        pending.pop((p, "c")).wait()
+
+def all_reduce(g, cid=1):
+    S = Stream(g.shape[0], g.shape[1])
+    return pl.pallas_call(functools.partial(ar_kernel, S), out_shape=jax.ShapeDtypeStruct(g.shape, g.dtype),
+        in_specs=[pl.BlockSpec(memory_space=pl.ANY)], out_specs=pl.BlockSpec(memory_space=pl.ANY),
+        scratch_shapes=S.scratch(),
+        compiler_params=pltpu.CompilerParams(collective_id=cid, has_side_effects=True, vmem_limit_bytes=60*2**20))(g)
+
 
 HEADS = 12
 HEAD_DIM = 64
@@ -245,23 +389,27 @@
         upstream = row_product(merged_grad, qkv_weight[depth]) + sum_grad
     input_grad = upstream.astype(jnp.bfloat16).reshape(hidden.shape)
     stacked = [jnp.stack([per_depth[0][member]]) for member in range(12)]
-    stacked = lax.psum(
-        (
-            stacked[0],
-            stacked[1],
-            stacked[2],
-            stacked[3],
-            stacked[4],
-            stacked[5],
-            stacked[6],
-            stacked[7],
-            stacked[8],
-            stacked[9],
-            stacked[10],
-            stacked[11],
-        ),
-        ("mod", "batch"),
-    )
+    def blocks(matrix):
+        rows, columns = matrix.shape
+        cut = matrix.astype(jnp.bfloat16).reshape(rows // 768, 768, columns // LANES, LANES)
+        return cut.transpose(0, 2, 1, 3).reshape(-1, 768, LANES)
+
+    def unblock(cut, rows, columns):
+        cut = cut.reshape(rows // 768, columns // LANES, 768, LANES).transpose(0, 2, 1, 3)
+        return cut.reshape(1, rows, columns).astype(jnp.float32)
+
+    small = [1, 3, 4, 5, 7, 9, 10, 11]
+    summed = lax.psum(tuple(stacked[i] for i in small), ("mod", "batch"))
+    for i, value in zip(small, summed):
+        stacked[i] = value
+    shapes = {0: (768, 2304), 2: (768, 768), 6: (768, 3072), 8: (3072, 768)}
+    packed = jnp.concatenate([blocks(stacked[i][0]) for i in shapes], 0)
+    packed = all_reduce(packed)
+    start = 0
+    for i, (rows, columns) in shapes.items():
+        count = rows * columns // (768 * LANES)
+        stacked[i] = unblock(packed[start : start + count], rows, columns)
+        start += count
     return (
         layer_out,
         input_grad,

time: 576 us -> 607 us (1.054)
  waiting for transfers between devices: 221 us -> 34.6 us
  Pallas kernels: 0 us -> 103 us
  local copies, waits for them, and re-layouts: 94.2 us -> 191 us
  other arithmetic: 30.2 us -> 64.9 us
  between operations: 15.3 us -> 1.53 us
  blocking collectives: 70.7 us -> 64.6 us
    psum x1 -> x0, waiting for transfers between devices: 154 us -> none  [body(): lax.psum((stacked[0], stacked[1], stacked[2], stacked[3], stacked[4], sta...]
    pallas_call x0 -> x1, Pallas kernels: none -> 103 us  [all_reduce(): pl.pallas_call(functools.partial(ar_kernel, S), out_shape=jax.ShapeDtypeS...]
    convert_element_type x0 -> x7, local copies, waits for them, and re-layouts: none -> 55.2 us  [the longest x5 41.9 us: unblock(): return cut.reshape(1, rows, columns).astype(jnp.float32)]
    ppermute x4, waiting for transfers between devices: 66.7 us -> 34.6 us  [partner(): lax.ppermute(x, axis, [(i, i ^ 1 << distance) for i in range(lax.axis_siz...]
    reshape x0 -> x4, local copies, waits for them, and re-layouts: none -> 24.6 us  [blocks(): matrix.astype(jnp.bfloat16)]
    concatenate x0 -> x1, other arithmetic: none -> 12.9 us  [body(): packed = jnp.concatenate([blocks(stacked[i][0]) for i in shapes], 0)]
    slice x0 -> x1, other arithmetic: none -> 10.4 us  [body(): stacked[i] = unblock(packed[start:start + count], rows, columns)]
    convert_element_type x0 -> x2, other arithmetic: none -> 8.55 us  [unblock(): return cut.reshape(1, rows, columns).astype(jnp.float32)]
  transfers between devices with their start and end apart: 5 -> 4, of which waited for: 5 -> 2; matrix products, arithmetic and copies ran while one was open for 12% -> 19% of each run, Pallas kernels for 0% -> 0%
where the time goes in v1:
time: 607 us; the launch traced here: 601 us
  local copies, waits for them, and re-layouts  191 us (31%)
  matrix products  135 us (22%)
  Pallas kernels  103 us (17%)
  other arithmetic  64.9 us (11%)
  blocking collectives  64.6 us (11%)
  waiting for transfers between devices  34.6 us (6%)
  starting transfers between devices  7.26 us (1%)
    pallas_call x1, Pallas kernels, all_reduce(): pl.pallas_call(functools.partial(ar_kernel, S), out_shape=jax.ShapeDtypeS...  103 us
    psum x1, blocking collectives, body(): summed = lax.psum(tuple((stacked[i] for i in small)), ('mod', 'batch'))  64.6 us
    unnamed x104, local copies, waits for them, and re-layouts  44.9 us
    convert_element_type x5, local copies, waits for them, and re-layouts, unblock(): return cut.reshape(1, rows, columns).astype(jnp.float32)  41.9 us
    ppermute x4, waiting for transfers between devices, partner(): lax.ppermute(x, axis, [(i, i ^ 1 << distance) for i in range(lax.axis_siz...  34.6 us
    dot_general x4, matrix products, row_product(): lax.dot_general(left, right, (((1,), (1,)), ((), ())), preferred_element_...  32.5 us
    dot_general x1, matrix products, body(): jnp.dot(first_low, up_weight[depth], preferred_element_type=jnp.float32)  31.3 us
    reshape x4, local copies, waits for them, and re-layouts, blocks(): matrix.astype(jnp.bfloat16)  24.6 us
  transfers between devices with their start and end apart: 4, of which 2 were waited for; matrix products, arithmetic and copies ran while one was open for 19% of the time, Pallas kernels for 0%

profile of v1, /device:TPU:1, one launch (start us, length us, event | category | flops | bytes accessed | tf_op | source)
XLA Modules:
  0.0 601.2 jit_solution(5432295296542722404)
XLA Ops:
  2.7 5.3 add_convert_fusion.1
  53.1 19.8 %collective-permute-done = bf16[896,768]{1,0:T(8,128)(2,1)} collective-permute-done((bf16[896,768]{1,0:T(8,128)(2,1)}, bf16[896,768]{1,0:T(8,128)(2,1)}, u32[]{:S(2)}, u32[]{:S(2)}) %collective-permute-start) | collective-permute-done | bytes 1376288 | tf_op jit(solution)/shard_map/ppermute | solution.py:161
  82.5 4.8 fusion.6
  101.7 31.3 %multiply_convert_fusion.1 = (bf16[896,3072]{1,0:T(8,128)(2,1)S(1)}, f32[896,3072]{1,0:T(8,128)}, f32[896,3072]{1,0:T(8,128)}) fusion(f32[3072]{0:T(1024)S(1)} %bitcast.191, bf16[1,768,3072]{2,1,0:T(8,128)(2,1)S(1)} %bitcast.197, f32[896,768]{1,0:T(8,128)S(1)} %get-tuple-element.82, f32[768]{0:T(1024)S(1)} %copy-done.26, f32[768]{0:T(1024)S(1)} %get-tuple-element.92, ...), kind=kOutput, calls=%fused_computation.7 | convolution fusion | flops 4412964864 | bytes 35021824 | tf_op jit(solution)/shard_map/dot_general | solution.py:258
  143.6 7.0 %convolution_convert_fusion = bf16[3072,768]{1,0:T(8,128)(2,1)} fusion(bf16[896,3072]{1,0:T(8,128)(2,1)S(1)} %get-tuple-element.65, bf16[896,768]{1,0:T(8,128)(2,1)S(1)} %get-tuple-element.58), kind=kOutput, calls=%fused_computation.31 | convolution fusion | flops 4230217728 | bytes 11599872 | tf_op jit(solution)/shard_map/dot_general | solution.py:171
  150.6 15.5 %convert_reduce_fusion = (f32[3072]{0:T(1024)}, bf16[896,3072]{1,0:T(8,128)(2,1)}) fusion(f32[896,3072]{1,0:T(8,128)} %get-tuple-element.66, bf16[896,768]{1,0:T(8,128)(2,1)S(1)} %get-tuple-element.58, bf16[1,3072,768]{2,1,0:T(8,128)(2,1)} %param.27, f32[896,3072]{1,0:T(8,128)} %get-tuple-element.83, f32[3072]{0:T(1024)S(1)} %bitcast.192), kind=kOutput, calls=%fused_computation.3 | convolution fusion | flops 4274648064 | bytes 33644544 | tf_op jit(solution)/shard_map/dot_general | solution.py:177
  166.1 9.8 %multiply_reduce_fusion.3 = (f32[768]{0:T(1024)}, f32[896]{0:T(1024)S(1)}, f32[768]{0:T(1024)}, f32[896,768]{1,0:T(8,128)S(1)}) fusion(f32[896,768]{1,0:T(8,128)S(1)} %get-tuple-element.82, f32[896]{0:T(1024)S(1)} %fusion.49, f32[896]{0:T(1024)S(1)} %broadcast_multiply_fusion.1, f32[768]{0:T(1024)S(1)} %get-tuple-element.92, ...), kind=kOutput, calls=%fused_computation.57 | convolution fusion | flops 4234737408 | bytes 18504704 | tf_op jit(solution)/shard_map/dot_general | solution.py:177
  175.9 7.8 %convolution_convert_fusion.1 = bf16[768,3072]{1,0:T(8,128)(2,1)} fusion(bf16[896,3072]{1,0:T(8,128)(2,1)S(1)} %copy-done.38, f32[896,768]{1,0:T(8,128)S(1)} %get-tuple-element.82, f32[768]{0:T(1024)S(1)} %copy-done.26, f32[768]{0:T(1024)S(1)} %get-tuple-element.92, f32[896]{0:T(1024)S(1)} %fusion.49, f32[896]{0:T(1024)S(1)} %broadcast_multiply_fusion.1), kind=kOutput, calls=%fused_computation.32 | convolution fusion | flops 4233658368 | bytes 12989440 | tf_op jit(solution)/shard_map/dot_general | solution.py:171
  196.6 6.2 %convolution_bitcast_fusion = f32[7,256,12,64]{1,3,2,0:T(8,128)S(1)} fusion(bf16[7,128,12,64]{1,0,3,2:T(8,128)(2,1)} %reshape.315, f32[7,12,128,256]{3,2,1,0:T(8,128)} %copy-done.1, f32[7,12,128]{2,1,0:T(8,128)} %copy-done.17, pred[7,256]{1,0:T(8,128)(4,1)S(1)} %copy-done.20), kind=kOutput, calls=%fused_computation.73 | convolution fusion | flops 363331584 | bytes 17936128 | tf_op jit(solution)/shard_map/phqk,pqhe->pkhe/dot_general | solution.py:351
  202.8 12.3 %multiply_reduce_fusion = (f32[7,12,128]{2,1,0:T(8,128)S(1)}, f32[7,12,128,256]{3,2,1,0:T(8,128)}) fusion(f32[7,12,128,256]{3,2,1,0:T(8,128)} %copy-done.1, f32[7,12,128]{2,1,0:T(8,128)S(1)} %copy-done.18, pred[7,256]{1,0:T(8,128)(4,1)S(1)} %copy-done.20, bf16[7,256,12,64]{1,3,2,0:T(8,128)(2,1)} %copy-done.13, bf16[7,128,12,64]{1,0,3,2:T(8,128)(2,1)S(1)} %copy-done.4), kind=kOutput, calls=%fused_computation.5 | convolution fusion | flops 366073344 | bytes 26236672 | tf_op jit(solution)/shard_map/pqhe,pkhe->phqk/dot_general | solution.py:348
  219.7 7.9 %multiply_convert_fusion = bf16[7,12,128,256]{3,2,1,0:T(8,128)(2,1)S(1)} fusion(f32[7,12,128,256]{3,2,1,0:T(8,128)} %get-tuple-element.88, f32[7,12,128,256]{3,2,1,0:T(8,128)S(1)} %bitcast.169, f32[7,12,128]{2,1,0:T(8,128)S(1)} %get-tuple-element.87, f32[7,12,128]{2,1,0:T(8,128)S(1)} %copy-done.18, pred[7,256]{1,0:T(8,128)(4,1)S(1)} %copy-done.20), kind=kLoop, calls=%fused_computation.4 | loop fusion | flops 16515072 | bytes 27612928 | tf_op jit(solution)/shard_map/convert_element_type | solution.py:357
  232.9 6.6 %copy.64 = bf16[3072,768]{0,1:T(8,128)(2,1)} copy(bf16[3072,768]{1,0:T(8,128)(2,1)} %convolution_convert_fusion) | data formatting | bytes 9437184 | tf_op jit(solution)/shard_map/convert_element_type | solution.py:394
  239.5 9.7 %reshape.326 = bf16[4,768,6,128]{1,0,3,2:T(4,128)(2,1)} reshape(bf16[3072,768]{0,1:T(8,128)(2,1)} %copy.64) | data formatting | bytes 9437184 | tf_op jit(solution)/shard_map/reshape | solution.py:394
  249.2 8.4 %copy.65 = bf16[4,6,768,128]{3,2,1,0:T(8,128)(2,1)} copy(bf16[4,6,768,128]{2,0,3,1:T(4,128)(2,1)} %bitcast.178) | data formatting | bytes 9437184 | tf_op jit(solution)/shard_map/transpose | solution.py:395
  257.6 6.6 %copy.62 = bf16[768,3072]{0,1:T(8,128)(2,1)} copy(bf16[768,3072]{1,0:T(8,128)(2,1)} %convolution_convert_fusion.1) | data formatting | bytes 9437184 | tf_op jit(solution)/shard_map/convert_element_type | solution.py:394
  264.3 6.6 %copy.63 = bf16[1,768,24,128]{3,1,2,0:T(8,128)(2,1)} copy(bf16[1,768,24,128]{1,3,2,0:T(8,128)(2,1)} %bitcast.179) | data formatting | bytes 9437184 | tf_op jit(solution)/shard_map/reshape | solution.py:394
  282.4 5.4 fusion.31
  293.1 14.8 %collective-permute-done.2 = bf16[7,128,12,64]{1,3,2,0:T(8,128)(2,1)} collective-permute-done((bf16[7,128,12,64]{1,3,2,0:T(8,128)(2,1)}, bf16[7,128,12,64]{1,3,2,0:T(8,128)(2,1)}, u32[]{:S(2)}, u32[]{:S(2)}) %collective-permute-start.2) | collective-permute-done | bytes 1376288 | tf_op jit(solution)/shard_map/ppermute | solution.py:161
  318.7 5.2 convolution_convert_fusion.2
  323.9 5.9 copy.60
  329.8 12.9 %pad_maximum_fusion.g_ref = bf16[72,768,128]{2,1,0:T(8,128)(2,1)} fusion(bf16[24,768,128]{2,1,0:T(8,128)(2,1)} %bitcast.175, bf16[24,768,128]{2,1,0:T(8,128)(2,1)} %bitcast.176, bf16[6,768,128]{2,1,0:T(8,128)(2,1)} %bitcast.185, bf16[18,768,128]{2,1,0:T(8,128)(2,1)} %bitcast.180), kind=kLoop, calls=%fused_computation.1 | loop fusion | flops 21233664 | bytes 28311552 | tf_op jit(solution)/shard_map/concatenate | solution.py:406
  342.7 102.6 %shard_map.263 = bf16[72,768,128]{2,1,0:T(8,128)(2,1)} custom-call(bf16[72,768,128]{2,1,0:T(8,128)(2,1)} %pad_maximum_fusion.g_ref), custom_call_target="tpu_custom_call" | custom-call | tf_op jit(solution)/shard_map/pallas_call | solution.py:146
  448.1 5.7 convert_bitcast_fusion.1
  453.8 10.4 %fusion.61 = (bf16[24,768,128]{2,1,0:T(8,128)(2,1)}, f32[1,768,24,128]{3,1,2,0:T(8,128)}) fusion(bf16[72,768,128]{2,1,0:T(8,128)(2,1)} %shard_map.263), kind=kLoop, calls=%fused_computation.135 | loop fusion | flops 2359296 | bytes 23592960 | tf_op jit(solution)/shard_map/slice | solution.py:411
  470.4 8.0 %copy.66 = f32[1,768,18,128]{1,3,2,0:T(8,128)} copy(f32[1,768,18,128]{3,1,2,0:T(8,128)} %convert_bitcast_fusion.1) | data formatting | bytes 14155776 | tf_op jit(solution)/shard_map/convert_element_type | solution.py:399
  478.4 8.0 %copy.72 = f32[1,768,2304]{2,1,0:T(8,128)} copy(f32[1,768,2304]{1,2,0:T(8,128)} %bitcast.172) | data formatting | bytes 14155776
  486.3 9.0 %copy.69 = f32[4,6,768,128]{2,0,3,1:T(4,128)} copy(bf16[4,6,768,128]{3,2,1,0:T(8,128)(2,1)} %bitcast.177) | data formatting | bytes 14155776 | tf_op jit(solution)/shard_map/convert_element_type | solution.py:399
  495.3 12.3 %reshape.346 = f32[1,3072,768]{1,2,0:T(8,128)} reshape(f32[4,768,6,128]{1,0,3,2:T(4,128)} %bitcast.170) | data formatting | bytes 18874368 | tf_op jit(solution)/shard_map/convert_element_type | solution.py:399
  507.6 9.6 %copy.75 = f32[1,3072,768]{2,1,0:T(8,128)} copy(f32[1,3072,768]{1,2,0:T(8,128)} %reshape.346) | data formatting | bytes 18874368
  517.2 9.6 %copy.68 = f32[1,768,24,128]{1,3,2,0:T(8,128)} copy(f32[1,768,24,128]{3,1,2,0:T(8,128)} %get-tuple-element.68) | data formatting | bytes 18874368 | tf_op jit(solution)/shard_map/convert_element_type | solution.py:399
  526.8 9.6 %copy.74 = f32[1,768,3072]{2,1,0:T(8,128)} copy(f32[1,768,3072]{1,2,0:T(8,128)} %bitcast.171) | data formatting | bytes 18874368
  536.4 64.6 %all-reduce = (f32[1,1536]{1,0:T(1,128)}, f32[1,768]{1,0:T(1,128)}, f32[1,768]{1,0:T(1,128)}, f32[1,768]{1,0:T(1,128)}, f32[1,3072]{1,0:T(1,128)}, /*index=5*/f3...) all-reduce(f32[1,1536]{1,0:T(1,128)S(1)} %stack.16, ...), channel_id=1, replica_groups=mesh['mod'=2,'batch'=64] {'mod','batch'}, use_global_device_ids=true, to_apply=%region_12.13 | all-reduce | flops 9216 | bytes 73728 | tf_op jit(solution)/shard_map/psum | solution.py:402
  (185 shorter events, 140.4 us)
Async XLA Ops:
  8.0 5.8 copy-start.33
  8.0 5.8 copy-start.34
  10.1 36.5 %collective-permute-start.1 = (bf16[896,768]{1,0:T(8,128)(2,1)}, bf16[896,768]{1,0:T(8,128)(2,1)}, u32[]{:S(2)}, u32[]{:S(2)}) collective-permute-start(bf16[896,768]{1,0:T(8,128)(2,1)} %get-tuple-element.70), channel_id=1, source_target_pairs={{0,64},{64,0},{1,65},{65,1},{2,66},{66,2},{3,67},{67,3},{4,68},{68... | collective-permute-start | bytes 4128776 | tf_op jit(solution)/shard_map/ppermute | solution.py:161
  13.7 59.2 %collective-permute-start = (bf16[896,768]{1,0:T(8,128)(2,1)}, bf16[896,768]{1,0:T(8,128)(2,1)}, u32[]{:S(2)}, u32[]{:S(2)}) collective-permute-start(bf16[896,768]{1,0:T(8,128)(2,1)} %get-tuple-element.71), channel_id=1, source_target_pairs={{0,64},{64,0},{1,65},{65,1},{2,66},{66,2},{3,67},{67,3},{4,68},{68... | collective-permute-start | bytes 4128776 | tf_op jit(solution)/shard_map/ppermute | solution.py:161
  29.5 8.1 %copy-start.32 = (s32[7]{0:T(128)S(1)}, s32[7]{0:T(128)}, u32[]{:S(2)}) copy-start(s32[7]{0:T(128)} %get-tuple-element.76) | copy-start | bytes 88
  29.5 8.1 %copy-start.31 = (bf16[1,768]{1,0:T(2,128)(2,1)S(1)}, bf16[1,768]{1,0:T(2,128)(2,1)}, u32[]{:S(2)}) copy-start(bf16[1,768]{1,0:T(2,128)(2,1)} %param.22) | copy-start | bytes 4612
  37.6 7.5 %copy-start.10 = (bf16[7,128,12,64]{1,0,3,2:T(8,128)(2,1)S(1)}, bf16[7,128,12,64]{1,0,3,2:T(8,128)(2,1)}, u32[]{:S(2)}) copy-start(bf16[7,128,12,64]{1,0,3,2:T(8,128)(2,1)} %reshape.309) | copy-start | bytes 4128772
  37.7 55.7 %copy-start.19 = (pred[7,256]{1,0:T(8,128)(4,1)}, pred[7,256]{1,0:T(8,128)(4,1)S(1)}, u32[]{:S(2)}) copy-start(pred[7,256]{1,0:T(8,128)(4,1)S(1)} %maximum_compare_fusion) | copy-start | bytes 5380
  87.3 6.1 %copy-start.1 = (f32[7,12,128,256]{3,2,1,0:T(8,128)}, f32[7,12,128,256]{3,2,1,0:T(8,128)S(1)}, u32[]{:S(2)}) copy-start(f32[7,12,128,256]{3,2,1,0:T(8,128)S(1)} %get-tuple-element.80) | copy-start | bytes 33030148
  87.3 5.5 copy-start.12
  92.8 4.2 copy-start.17
  98.7 34.3 %slice-start.5 = ((s8[4718592]{0:T(1024)(128)(4,1)}), s8[4194304]{0:T(1024)(128)(4,1)S(1)}, s32[]{:S(2)}) async-start(s8[4718592]{0:T(1024)(128)(4,1)} %bitcast.194), calls=%async_computation.5 | async-start | bytes 8388608
  101.7 31.3 %copy-start.29 = (f32[768]{0:T(1024)S(1)}, f32[768]{0:T(1024)}, u32[]{:S(2)}) copy-start(f32[768]{0:T(1024)} %convert_reduce_fusion.6) | copy-start | bytes 9220
  101.7 31.3 %slice-start.6 = ((s8[4718592]{0:T(1024)(128)(4,1)}), s8[524288]{0:T(1024)(128)(4,1)S(1)}, s32[]{:S(2)}) async-start(s8[4718592]{0:T(1024)(128)(4,1)} %bitcast.194), calls=%async_computation.6 | async-start | bytes 1048576
  166.1 9.8 %copy-start.38 = (bf16[896,3072]{1,0:T(8,128)(2,1)S(1)}, bf16[896,3072]{1,0:T(8,128)(2,1)}, u32[]{:S(2)}) copy-start(bf16[896,3072]{1,0:T(8,128)(2,1)} %get-tuple-element.90) | copy-start | bytes 16515076
  190.0 6.5 %copy-start.20 = (pred[7,256]{1,0:T(8,128)(4,1)S(1)}, pred[7,256]{1,0:T(8,128)(4,1)}, u32[]{:S(2)}) copy-start(pred[7,256]{1,0:T(8,128)(4,1)} %copy-done.19) | copy-start | bytes 5380
  196.6 6.2 %copy-start.4 = (bf16[7,128,12,64]{1,0,3,2:T(8,128)(2,1)S(1)}, bf16[7,128,12,64]{1,0,3,2:T(8,128)(2,1)}, u32[]{:S(2)}) copy-start(bf16[7,128,12,64]{1,0,3,2:T(8,128)(2,1)} %reshape.315) | copy-start | bytes 4128772
  196.6 6.2 %copy-start.18 = (f32[7,12,128]{2,1,0:T(8,128)S(1)}, f32[7,12,128]{2,1,0:T(8,128)}, u32[]{:S(2)}) copy-start(f32[7,12,128]{2,1,0:T(8,128)} %copy-done.17) | copy-start | bytes 129028
  196.6 23.1 %slice-start = ((s8[11010048]{0:T(1024)(128)(4,1)}), s8[4194304]{0:T(1024)(128)(4,1)S(1)}, s32[]{:S(2)}) async-start(s8[11010048]{0:T(1024)(128)(4,1)} %bitcast.168), calls=%async_computation | async-start | bytes 8388608
  196.6 23.0 %slice-start.1 = ((s8[11010048]{0:T(1024)(128)(4,1)}), s8[4194304]{0:T(1024)(128)(4,1)S(1)}, s32[]{:S(2)}) async-start(s8[11010048]{0:T(1024)(128)(4,1)} %bitcast.168), calls=%async_computation.1 | async-start | bytes 8388608
  202.8 12.3 %copy-start.3 = (f32[7,256,12,64]{1,3,2,0:T(8,128)}, f32[7,256,12,64]{1,3,2,0:T(8,128)S(1)}, u32[]{:S(2)}) copy-start(f32[7,256,12,64]{1,3,2,0:T(8,128)S(1)} %convolution_bitcast_fusion) | copy-start | bytes 16515076
  202.8 16.8 %slice-start.2 = ((s8[11010048]{0:T(1024)(128)(4,1)}), s8[2621440]{0:T(1024)(128)(4,1)S(1)}, s32[]{:S(2)}) async-start(s8[11010048]{0:T(1024)(128)(4,1)} %bitcast.168), calls=%async_computation.2 | async-start | bytes 5242880
  216.5 72.7 %collective-permute-start.3 = (bf16[7,128,12,64]{1,3,2,0:T(8,128)(2,1)}, bf16[7,128,12,64]{1,3,2,0:T(8,128)(2,1)}, u32[]{:S(2)}, u32[]{:S(2)}) collective-permute-start(bf16[7,128,12,64]{1,3,2,0:T(8,128)(2,1)} %slice.87), channel_id=1, source_target_pairs={{0,64},{64,0},{1,65},{65,1},{2,66},{66,2},{3,67},{67,3},{4,68},{68... | collective-permute-start | bytes 4128776 | tf_op jit(solution)/shard_map/ppermute | solution.py:161
  219.6 7.9 %copy-start.6 = (bf16[7,128,12,64]{1,0,3,2:T(8,128)(2,1)S(1)}, bf16[7,128,12,64]{1,0,3,2:T(8,128)(2,1)}, u32[]{:S(2)}) copy-start(bf16[7,128,12,64]{1,0,3,2:T(8,128)(2,1)} %reshape.311) | copy-start | bytes 4128772
  264.3 6.6 %copy-start.28 = (f32[768]{0:T(1024)S(1)}, f32[768]{0:T(1024)}, u32[]{:S(2)}) copy-start(f32[768]{0:T(1024)} %get-tuple-element.42) | copy-start | bytes 9220
  264.3 7.2 %copy-start.27 = (f32[768]{0:T(1024)S(1)}, f32[768]{0:T(1024)}, u32[]{:S(2)}) copy-start(f32[768]{0:T(1024)} %get-tuple-element.46) | copy-start | bytes 9220
  270.9 5.3 copy-start.15
  275.8 32.0 %collective-permute-start.2 = (bf16[7,128,12,64]{1,3,2,0:T(8,128)(2,1)}, bf16[7,128,12,64]{1,3,2,0:T(8,128)(2,1)}, u32[]{:S(2)}, u32[]{:S(2)}) collective-permute-start(bf16[7,128,12,64]{1,3,2,0:T(8,128)(2,1)} %slice.88), channel_id=1, source_target_pairs={{0,64},{64,0},{1,65},{65,1},{2,66},{66,2},{3,67},{67,3},{4,68},{68... | collective-permute-start | bytes 4128776 | tf_op jit(solution)/shard_map/ppermute | solution.py:161
  288.9 19.0 %slice-start.3 = ((s8[5505024]{0:T(1024)(128)(4,1)}), s8[4194304]{0:T(1024)(128)(4,1)S(1)}, s32[]{:S(2)}) async-start(s8[5505024]{0:T(1024)(128)(4,1)} %bitcast.173), calls=%async_computation.3 | async-start | bytes 8388608
  289.2 18.7 %slice-start.4 = ((s8[5505024]{0:T(1024)(128)(4,1)}), s8[1310720]{0:T(1024)(128)(4,1)S(1)}, s32[]{:S(2)}) async-start(s8[5505024]{0:T(1024)(128)(4,1)} %bitcast.173), calls=%async_computation.4 | async-start | bytes 2621440
  526.8 9.6 %copy-start.23 = (f32[1,768]{1,0:T(1,128)S(1)}, f32[1,768]{1,0:T(1,128)}, u32[]{:S(2)}) copy-start(f32[1,768]{1,0:T(1,128)} %reshape.331) | copy-start | bytes 9220
  526.8 9.6 %copy-start.24 = (f32[1,768]{1,0:T(1,128)S(1)}, f32[1,768]{1,0:T(1,128)}, u32[]{:S(2)}) copy-start(f32[1,768]{1,0:T(1,128)} %reshape.330) | copy-start | bytes 9220
  (20 other events, 45.1 us)

commit v2 on v1

v2 whole, which is shorter than its diff:
```python
import functools
import math

import jax
import jax.numpy as jnp
from jax import lax
from jax.experimental import pallas as pl
from jax.experimental.pallas import tpu as pltpu
from jax.sharding import PartitionSpec as P

MESH = pl.DeviceIdType.MESH

BF, F32 = jnp.bfloat16, jnp.float32
LANES = 128
D, HEADS, FF, SLOTS = 768, 12, 3072, 128
WHOLE = 3
QROWS = WHOLE * 256 + 128
KROWS = QROWS + 128
EPS = 1e-6
MASKED = -1e9
LOG2E = math.log2(math.e)
SCALE = 0.125
UF, UB, GT, LR, LU = 6, 3, 768, 128, 1

def nn(a, b):
    return lax.dot_general(a, b, (((1,), (0,)), ((), ())), preferred_element_type=F32)
def nt(a, b):
    return lax.dot_general(a, b, (((1,), (1,)), ((), ())), preferred_element_type=F32)
def tn(a, b):
    return lax.dot_general(a, b, (((0,), (0,)), ((), ())), preferred_element_type=F32)

def gelu_pair(v):
    a = jnp.abs(v)
    e = jnp.exp2(v * v * (-0.5 * LOG2E))
    d = 1.0 + (0.3275911 / math.sqrt(2.0)) * a
    t = pl.reciprocal(d, approx=True)
    t = t * (2.0 - d * t)
    poly = ((((0.5 * 1.061405429 * t + 0.5 * -1.453152027) * t + 0.5 * 1.421413741) * t + 0.5 * -0.284496736) * t + 0.5 * 0.254829592) * t
    tail = poly * e
    cdf = jnp.where(v >= 0, 1.0 - tail, tail)
    return v * cdf, cdf + v * e * (1.0 / math.sqrt(2.0 * math.pi))

VEC = dict(q=0, v=768, out=1536, g1=2304, b1=3072, up=3840, down=6912, g2=7680, b2=8448)
VLEN = 9216

def normalize(s):
    centre = s - jnp.mean(s, -1, keepdims=True)
    r = lax.rsqrt(jnp.mean(centre * centre, -1, keepdims=True) + EPS)
    return centre * r, r

def norm_back(g, n, r):
    return r * (g - jnp.mean(g, -1, keepdims=True) - n * jnp.mean(g * n, -1, keepdims=True))

def compute_kernel(stop, hid, rhid, og, rog, tc, rc, wqkv_h, qvb, wo_h, bo_l, g1_l, b1_l, wup_h, bup_l, wdn_h, bdn_l, g2_l, b2_l,
                   y_ref, yo_ref, ig_ref, igo_ref, mid_ref, grad_ref, vec,
                   x, xt, merged, ctx, fsum, flow, flowt, act, pre, branch, dsec, mid32,
                   wqkv, wo, wup, wdn, ogv, stage, bqkv, bup, small, colsum, wsem, iosem, gsem):
    mod = lax.axis_index("mod")
    bqkv[:, 0:768] = qvb[:, 0:768].astype(F32)
    bqkv[:, 768:1536] = jnp.zeros((1, 768), F32)
    bqkv[:, 1536:2304] = qvb[:, 768:1536].astype(F32)
    bup[...] = bup_l[...].astype(F32)
    for k, l in enumerate((bo_l, g1_l, b1_l, bdn_l, g2_l, b2_l)):
        small[k] = l[...].astype(F32)
    bo, g1, b1, bdn, g2, b2 = (small.at[k] for k in range(6))
    def pair_of(i):
        return i + mod * (6 - 2 * i)
    def recv_of(i, n):
        return i + mod * (n - 1 - 2 * i)
    loads = []
    for k, (src, dst) in enumerate([(wqkv_h, wqkv), (wo_h, wo), (wup_h, wup), (wdn_h, wdn)]):
        loads.append(pltpu.make_async_copy(src, dst, wsem.at[k]))
    xin = []
    for i in range(4):
        xin.append(pltpu.make_async_copy(hid.at[pair_of(i)], x.at[pl.ds(i * 256, 128)], iosem.at[i]))
        xin.append(pltpu.make_async_copy(rhid.at[recv_of(i, 4)], x.at[pl.ds(i * 256 + 128, 128)], iosem.at[4 + i]))
    ogin = []
    for i in range(4):
        ogin.append(pltpu.make_async_copy(og.at[pair_of(i)], ogv.at[pl.ds(i * 256, 128)], iosem.at[8 + i]))
        if i < 3:
            ogin.append(pltpu.make_async_copy(rog.at[recv_of(i, 3)], ogv.at[pl.ds(i * 256 + 128, 128)], iosem.at[12 + i]))
    for c in xin: c.start()
    loads[0].start()
    for c in loads[1:]: c.start()
    for c in ogin: c.start()
    for c in xin: c.wait()
    loads[0].wait()

    def own_count(i):
        return jnp.where(mod == 0, tc[pair_of(i)], rc[pair_of(i)])
    def other_count(i):
        return jnp.where(mod == 0, rc[pair_of(i)], tc[pair_of(i)])

    def p1(j, _):
        cols = pl.ds(pl.multiple_of(j * 768, 768), 768)
        merged[:, cols] = (nn(x[...], wqkv[:, cols]) + bqkv[:, cols]).astype(BF)
        return 0
    lax.fori_loop(0, 3, p1, 0)
    if stop <= 1:
        for c in loads[1:] + ogin: c.wait()
        return
    lane = lax.broadcasted_iota(jnp.int32, (256, 128), 1)
    row = lax.broadcasted_iota(jnp.int32, (256, 256), 0)
    def key_live(i, nq):
        r = lax.broadcasted_iota(jnp.int32, (256, nq), 0)
        return r < jnp.where(r < 128, own_count(i), 128 + other_count(i))
    zero = jnp.zeros((), BF)
    def half(v, h):
        l = lax.broadcasted_iota(jnp.int32, v.shape, 1)
        return jnp.where((l < 64) if h == 0 else (l >= 64), v, zero)
    def attend(i, hp, nq):
        base = pl.multiple_of(i * 256, 256)
        c0 = pl.multiple_of(hp * 128, 128)
        q = merged[pl.ds(base, nq), pl.ds(c0, 128)]
        k = merged[pl.ds(base, 256), pl.ds(c0 + 768, 128)]
        v = merged[pl.ds(base, 256), pl.ds(c0 + 1536, 128)]
        live = key_live(i, nq)
        out = None
        for h in range(2):
            s = nt(half(k, h), q) * (SCALE * LOG2E)
            s = jnp.where(live, s, MASKED)
            m = jnp.max(s, 0, keepdims=True)
            e = jnp.exp2(s - m)
            p = (e * (1.0 / jnp.sum(e, 0, keepdims=True))).astype(BF)
            o = tn(p, half(v, h))
            out = o if out is None else out + o
        ctx[pl.ds(base, nq), pl.ds(c0, 128)] = out.astype(BF)
    def p2(t, _):
        for u in range(UF): attend(t // (6 // UF), lax.rem(t, 6 // UF) * UF + u, 256)
        return 0
    lax.fori_loop(0, WHOLE * 6 // UF, p2, 0)
    def p2m(t, _):
        for u in range(UF): attend(WHOLE, t * UF + u, 128)
        return 0
    lax.fori_loop(0, 6 // UF, p2m, 0)
    if stop <= 2:
        for c in loads[1:] + ogin: c.wait()
        return
    loads[1].wait()
    fsum[...] = x[0:QROWS, :].astype(F32) + nn(ctx[...], wo[...]) + bo[...]
    def p3(r, _):
        rows = pl.ds(pl.multiple_of(r * LR, LR), LR)
        n, _r = normalize(fsum[rows, :])
        flow[rows, :] = (n * g1[...] + b1[...]).astype(BF)
        return 0
    lax.fori_loop(0, QROWS // LR, p3, 0, unroll=LU)
    if stop <= 3:
        for c in loads[2:] + ogin: c.wait()
        return
    loads[2].wait()
    def p4(j, _):
        cols = pl.ds(pl.multiple_of(j * GT, GT), GT)
        a, d = gelu_pair(nn(flow[...], wup[:, cols]) + bup[:, cols])
        act[:, cols] = a.astype(BF)
        pre[:, cols] = d.astype(BF)
        return 0
    lax.fori_loop(0, FF // GT, p4, 0)
    if stop <= 4:
        for c in loads[3:] + ogin: c.wait()
        return
    loads[3].wait()
    for c in ogin: c.wait()
    dsec[...] = nn(act[...], wdn[...]) + bdn[...]
    colsum[...] = jnp.zeros_like(colsum)
    def fold(v):
        return v.reshape(v.shape[0] // 8, 8, v.shape[1]).sum(0)
    def p5(r, _):
        rows = pl.ds(pl.multiple_of(r * LR, LR), LR)
        slot = r * LR // 128
        i = slot // 2
        live = lax.broadcasted_iota(jnp.int32, (LR, 1), 0) + lax.rem(r * LR, 128) < jnp.where(lax.rem(slot, 2) == 0, own_count(i), other_count(i))
        livef = live.astype(F32)
        n, rr = normalize(fsum[rows, :])
        n, rr = normalize(n * g1[...] + b1[...] + dsec[rows, :])
        dout = ogv[rows, :].astype(F32) * livef
        ogv[rows, :] = ((n * g2[...] + b2[...]) * livef).astype(BF)
        colsum[0] += fold(dout * n)
        colsum[1] += fold(dout)
        ds = norm_back(dout * g2[...], n, rr)
        dsec[rows, :] = ds
        low = ds.astype(BF)
        branch[rows, :] = low
        colsum[2] += fold(low.astype(F32))
        return 0
    lax.fori_loop(0, QROWS // LR, p5, 0, unroll=LU)
    for k, name in enumerate(("g2", "b2", "down")):
        vec[:, VEC[name]:VEC[name] + 768] = jnp.sum(colsum[k], 0, keepdims=True)
    outs = []
    for i in range(4):
        outs.append(pltpu.make_async_copy(ogv.at[pl.ds(i * 256, 128)], y_ref.at[pair_of(i)], iosem.at[i]))
        if i < 3:
            outs.append(pltpu.make_async_copy(ogv.at[pl.ds(i * 256 + 128, 128)], yo_ref.at[i + mod * (2 - 2 * i)], iosem.at[4 + i]))
    for c in outs: c.start()
    for c in outs: c.wait()
    if stop <= 5: return
    def gcopy(slot, block):
        return pltpu.make_async_copy(stage.at[slot], grad_ref.at[pl.ds(block, 6)], gsem.at[slot])
    def put(t, block, value, first):
        slot = lax.rem(t, 2)
        @pl.when(jnp.logical_not(first))
        def _(): gcopy(slot, block).wait()
        for b in range(6): stage[slot, b] = value[:, b * 128:(b + 1) * 128]
        gcopy(slot, block).start()
    def p6(t, _):
        rows = pl.ds(pl.multiple_of(t * 768, 768), 768)
        put(t, 24 + t * 6, tn(act[:, rows], branch[...]).astype(BF), t < 2)
        return 0
    lax.fori_loop(0, 4, p6, 0)
    if stop <= 6:
        for s in range(2): gcopy(s, 0).wait()
        return
    flowt[...] = flow[...].T
    def p7(j, _):
        cols = pl.ds(pl.multiple_of(j * 768, 768), 768)
        pg = nt(branch[...], wdn[cols, :]) * pre[:, cols].astype(F32)
        low = pg.astype(BF)
        pre[:, cols] = low
        vec[:, pl.ds(pl.multiple_of(VEC["up"] + j * 768, 768), 768)] = jnp.sum(low.astype(F32), 0, keepdims=True)
        put(j, 6 * j, nn(flowt[...], low).astype(BF), False)
        return 0
    lax.fori_loop(0, 4, p7, 0)
    if stop <= 7:
        for s in range(2): gcopy(s, 0).wait()
        return
    dsec[...] += nt(pre[...], wup[...])
    colsum[...] = jnp.zeros_like(colsum)
    def p8(r, _):
        rows = pl.ds(pl.multiple_of(r * LR, LR), LR)
        g = dsec[rows, :]
        n, rr = normalize(fsum[rows, :])
        colsum[0] += fold(g * n)
        colsum[1] += fold(g)
        df = norm_back(g * g1[...], n, rr)
        dsec[rows, :] = df
        low = df.astype(BF)
        branch[rows, :] = low
        colsum[2] += fold(low.astype(F32))
        return 0
    lax.fori_loop(0, QROWS // LR, p8, 0, unroll=LU)
    for k, name in enumerate(("g1", "b1", "out")):
        vec[:, VEC[name]:VEC[name] + 768] = jnp.sum(colsum[k], 0, keepdims=True)
    flow[...] = nt(branch[...], wo[...]).astype(BF)
    if stop <= 8:
        for s in range(2): gcopy(s, 0).wait()
        return
    put(0, 48, tn(ctx[...], branch[...]).astype(BF), False)
    if stop <= 9:
        for s in range(2): gcopy(s, 0).wait()
        return
    def attend_back(i, hp, nq):
        base = pl.multiple_of(i * 256, 256)
        c0 = pl.multiple_of(hp * 128, 128)
        qs, ks, vs = (pl.ds(c0 + 768 * m, 128) for m in range(3))
        q = merged[pl.ds(base, nq), qs]
        k = merged[pl.ds(base, 256), ks]
        v = merged[pl.ds(base, 256), vs]
        dc = flow[pl.ds(base, nq), pl.ds(c0, 128)]
        live = key_live(i, nq)
        dq = dk = dv = None
        for h in range(2):
            kh = half(k, h)
            s = nt(kh, q) * (SCALE * LOG2E)
            s = jnp.where(live, s, MASKED)
            m = jnp.max(s, 0, keepdims=True)
            e = jnp.exp2(s - m)
            p = e * (1.0 / jnp.sum(e, 0, keepdims=True))
            dp = nt(half(v, h), dc)
            ds = (p * (dp - jnp.sum(p * dp, 0, keepdims=True))).astype(BF)
            a, b, c = nn(p.astype(BF), half(dc, h)), nn(ds, half(q, h)), tn(ds, kh)
            if h == 0: dv, dk, dq = a, b, c
            else: dv, dk, dq = dv + a, dk + b, dq + c
        merged[pl.ds(base, nq), qs] = (dq * SCALE).astype(BF)
        merged[pl.ds(base, 256), ks] = (dk * SCALE).astype(BF)
        merged[pl.ds(base, 256), vs] = dv.astype(BF)
        if nq < 256:
            merged[pl.ds(base + nq, 256 - nq), qs] = jnp.zeros((256 - nq, 128), BF)
    def p10(t, _):
        for u in range(UB): attend_back(t // (6 // UB), lax.rem(t, 6 // UB) * UB + u, 256)
        return 0
    lax.fori_loop(0, WHOLE * 6 // UB, p10, 0)
    def p10m(t, _):
        for u in range(UB): attend_back(WHOLE, t * UB + u, 128)
        return 0
    lax.fori_loop(0, 6 // UB, p10m, 0)
    if stop <= 10:
        for s in range(2): gcopy(s, 0).wait()
        return
    xt[...] = x[...].T
    def p11(j, _):
        cols = pl.ds(pl.multiple_of(j * 768, 768), 768)
        mg = merged[:, cols]
        put(j + 1, 54 + 6 * j, nn(xt[...], mg).astype(BF), False)
        @pl.when(j != 1)
        def _(): vec[:, pl.ds(pl.multiple_of((j // 2) * 768, 768), 768)] = jnp.sum(mg.astype(F32), 0, keepdims=True)
        return 0
    lax.fori_loop(0, 3, p11, 0)
    for s in range(2): gcopy(s, 0).wait()
    if stop <= 11: return
    g = nt(merged[...], wqkv[...])
    x[0:768, :] = (g[0:768] + dsec[0:768, :]).astype(BF)
    mid32[...] = g[768:896] + dsec[768:896, :]
    x[896:, :] = g[896:].astype(BF)
    outs = []
    for i in range(4):
        if i < 3: outs.append(pltpu.make_async_copy(x.at[pl.ds(i * 256, 128)], ig_ref.at[pair_of(i)], iosem.at[i]))
        outs.append(pltpu.make_async_copy(x.at[pl.ds(i * 256 + 128, 128)], igo_ref.at[recv_of(i, 4)], iosem.at[4 + i]))
    outs.append(pltpu.make_async_copy(mid32, mid_ref, iosem.at[8]))
    for c in outs: c.start()
    for c in outs: c.wait()

def compute(stop, hid, rhid, og, rog, tc, rc, wqkv, qvb, wo, bo, g1, b1, wup, bup, wdn, bdn, g2, b2):
    any_, vm, sm_ = (pl.BlockSpec(memory_space=m) for m in (pl.ANY, pltpu.VMEM, pltpu.SMEM))
    S = jax.ShapeDtypeStruct
    return pl.pallas_call(functools.partial(compute_kernel, stop),
        out_shape=(S((7, 128, 768), BF), S((3, 128, 768), BF), S((7, 128, 768), BF), S((4, 128, 768), BF), S((128, 768), F32),
                   S((72, 768, 128), BF), S((1, VLEN), F32)),
        in_specs=[any_] * 4 + [sm_] * 2 + [any_, vm, any_, vm, vm, vm, any_, vm, any_, vm, vm, vm],
        out_specs=(any_,) * 6 + (vm,),
        scratch_shapes=[pltpu.VMEM((KROWS, D), BF), pltpu.VMEM((D, KROWS), BF), pltpu.VMEM((KROWS, 3 * D), BF), pltpu.VMEM((QROWS, D), BF),
            pltpu.VMEM((QROWS, D), F32), pltpu.VMEM((QROWS, D), BF), pltpu.VMEM((D, QROWS), BF), pltpu.VMEM((QROWS, FF), BF), pltpu.VMEM((QROWS, FF), BF),
            pltpu.VMEM((QROWS, D), BF), pltpu.VMEM((QROWS, D), F32), pltpu.VMEM((128, D), F32),
            pltpu.VMEM((D, 3 * D), BF), pltpu.VMEM((D, D), BF), pltpu.VMEM((D, FF), BF), pltpu.VMEM((FF, D), BF), pltpu.VMEM((QROWS, D), BF),
            pltpu.VMEM((2, 6, 768, 128), BF), pltpu.VMEM((1, 3 * D), F32), pltpu.VMEM((1, FF), F32), pltpu.VMEM((6, 1, D), F32), pltpu.VMEM((3, 8, D), F32),
            pltpu.SemaphoreType.DMA((4,)), pltpu.SemaphoreType.DMA((16,)), pltpu.SemaphoreType.DMA((2,))],
        compiler_params=pltpu.CompilerParams(vmem_limit_bytes=62 * 2**20),
        )(hid, rhid, og, rog, tc, rc, wqkv, qvb, wo, bo, g1, b1, wup, bup, wdn, bdn, g2, b2)


def place():
    mod, batch = lax.axis_index("mod"), lax.axis_index("batch")
    return mod * 2 + lax.rem(batch // 2, 2), batch // 16, lax.rem(batch // 4, 4), lax.rem(batch, 2)

def device(x, y, z, core):
    return (x // 2, y * 16 + z * 4 + lax.rem(x, 2) * 2 + core)

def near(v):
    return v + 1 - 2 * lax.rem(v, 2)

def neighbours():
    x, y, z, core = place()
    targets = [device(near(x), y, z, core), device(x, near(y), z, core), device(x, y, near(z), core),
               device(3 - x, y, z, core), device(x, 3 - y, z, core), device(x, y, 3 - z, core)]
    bits = [lax.rem((v + 1) // 2, 2) for v in (x, y, z)] + [v // 2 for v in (x, y, z)]
    return targets, bits, device(x, y, z, 1 - core), core

class Stream:
    def __init__(self, blocks, rows):
        self.blocks, self.rows = blocks, rows
        self.half = blocks // 2
        self.part = self.half // 6
        assert self.part % 2 == 0
        self.shapes = []
        r, b = rows, self.part
        for s in range(4):
            r //= 2
            self.shapes.append((b, r))
        b //= 2
        self.shapes.append((b, r))
        self.shapes.append((b, r))

    def scratch(self):
        return [pltpu.VMEM((self.half, self.rows, LANES), jnp.bfloat16),
                pltpu.VMEM((self.half, self.rows, LANES), jnp.bfloat16)] + [
                pltpu.VMEM((6, b, r, LANES), jnp.bfloat16) for b, r in self.shapes] + [
                pltpu.SemaphoreType.DMA((6, 8)), pltpu.SemaphoreType.DMA((6, 8)),
                pltpu.SemaphoreType.DMA((6, 6)), pltpu.SemaphoreType.DMA((6, 6))]

def ar_kernel(stream, g_ref, v_ref, o_ref, vo_ref, vbuf, vss, vrs, acc, corebuf, r0, r1, r2, r3, r4, r5, ssem, rsem, sag, rag):
    S = stream
    recv = [r0, r1, r2, r3, r4, r5]
    targets, bits, sibling, core = neighbours()
    bar = pltpu.get_barrier_semaphore()
    for t in targets + [sibling]:
        pl.semaphore_signal(bar, inc=1, device_id=t, device_id_type=MESH)
    pl.semaphore_wait(bar, 7)
    width = S.part
    def remote(src, dst, a, b, t):
        return pltpu.make_async_remote_copy(src, dst, a, b, device_id=t, device_id_type=MESH)
    cc, lc = [], []
    for p in range(6):
        c = remote(g_ref.at[pl.ds((1 - core) * S.half + p * width, width)], corebuf.at[pl.ds(p * width, width)], ssem.at[p, 0], rsem.at[p, 0], sibling)
        c.start(); cc.append(c)
        l = pltpu.make_async_copy(g_ref.at[pl.ds(core * S.half + p * width, width)], acc.at[pl.ds(p * width, width)], ssem.at[p, 7])
        l.start(); lc.append(l)
    reg = [[p * width, 0] for p in range(6)]
    cur = (width, S.rows)
    def add(dst, src, b, rows, chunk=48):
        n = rows // chunk
        def body(i, _):
            k, r = i // n, lax.rem(i, n) * chunk
            dst(k, r, chunk)[...] = dst(k, r, chunk)[...] + src(k, r, chunk)[...]
            return 0
        lax.fori_loop(0, b * n, body, 0)
    pending = {}
    def begin(p, s):
        b, r = S.shapes[s]
        d = (p + s) % 6
        bit = bits[d]
        bo, ro = reg[p]
        if s < 4:
            src = acc.at[pl.ds(bo, b), pl.ds(pl.multiple_of(ro + (1 - bit) * r, 16), r)]
            reg[p] = [bo, ro + bit * r]
        elif s == 4:
            src = acc.at[pl.ds(bo + (1 - bit) * b, b), pl.ds(pl.multiple_of(ro, 16), r)]
            reg[p] = [bo + bit * b, ro]
        else:
            src = acc.at[pl.ds(bo, b), pl.ds(pl.multiple_of(ro, 16), r)]
        c = remote(src, recv[s].at[p], ssem.at[p, s + 1], rsem.at[p, s + 1], targets[d])
        c.start()
        pending[p, s] = c
    def finish(p, s):
        b, r = S.shapes[s]
        bo, ro = reg[p]
        c = pending.pop((p, s))
        if s == 5: c.wait()
        else:
            c.wait_recv()
            c.wait_send()
        ch = 48
        add(lambda k, rr, n: acc.at[bo + k, pl.ds(pl.multiple_of(ro + rr, 16), n)], lambda k, rr, n: recv[s].at[p, k, pl.ds(pl.multiple_of(rr, 16), n)], b, r, ch)
    vo_ref[...] = v_ref[...]
    vcopy = {}
    def vbegin(s):
        vcopy[s] = remote(vo_ref, vbuf.at[s], vss.at[s], vrs.at[s], sibling if s == 0 else targets[s - 1])
        vcopy[s].start()
    def vfinish(s):
        vcopy[s].wait()
        vo_ref[...] = vo_ref[...] + vbuf[s]
    vbegin(0)
    for p in range(6):
        cc[p].wait(); lc[p].wait()
        add(lambda k, rr, n: acc.at[p * width + k, pl.ds(pl.multiple_of(rr, 16), n)], lambda k, rr, n: corebuf.at[p * width + k, pl.ds(pl.multiple_of(rr, 16), n)], width, S.rows, 192)
        begin(p, 0)
    for s in range(6):
        vfinish(s)
        vbegin(s + 1)
        for p in range(6):
            finish(p, s)
            if s < 5: begin(p, s + 1)
            else:
                b, r = S.shapes[5]
                bo, ro = reg[p]
                l = pltpu.make_async_copy(acc.at[pl.ds(bo, b), pl.ds(pl.multiple_of(ro, 16), r)],
                                          o_ref.at[pl.ds(core * S.half + bo, b), pl.ds(pl.multiple_of(ro, 16), r)], sag.at[p, 5])
                l.start(); pending[p, "l"] = l
    vfinish(6)
    def gather(p, s):
        b, r = S.shapes[s]
        bo, ro = reg[p]
        d = (p + s) % 6
        ref = o_ref.at[pl.ds(core * S.half + bo, b), pl.ds(pl.multiple_of(ro, 16), r)]
        c = remote(ref, ref, sag.at[p, s], rag.at[p, s], targets[d])
        c.start(); pending[p, s] = c
        bit = bits[d]
        if s == 4: reg[p] = [bo - bit * b, ro]
        else: reg[p] = [bo, ro - bit * r]
    for p in range(6):
        pending.pop((p, "l")).wait()
        gather(p, 4)
    for s in range(4, -1, -1):
        for p in range(6):
            pending.pop((p, s)).wait()
            if s > 0: gather(p, s - 1)
            else:
                ref = o_ref.at[pl.ds(core * S.half + p * width, width)]
                c = remote(ref, ref, ssem.at[p, 7], rag.at[p, 5], sibling)
                c.start(); pending[p, "c"] = c
    for p in range(6):
        pending.pop((p, "c")).wait()

def all_reduce(g, v, cid=1):
    S = Stream(g.shape[0], g.shape[1])
    return pl.pallas_call(functools.partial(ar_kernel, S),
        out_shape=(jax.ShapeDtypeStruct(g.shape, g.dtype), jax.ShapeDtypeStruct(v.shape, v.dtype)),
        in_specs=[pl.BlockSpec(memory_space=pl.ANY), pl.BlockSpec(memory_space=pltpu.VMEM)],
        out_specs=(pl.BlockSpec(memory_space=pl.ANY), pl.BlockSpec(memory_space=pltpu.VMEM)),
        scratch_shapes=[pltpu.VMEM((7,) + v.shape, v.dtype), pltpu.SemaphoreType.DMA((7,)), pltpu.SemaphoreType.DMA((7,))] + S.scratch(),
        compiler_params=pltpu.CompilerParams(collective_id=cid, has_side_effects=True, vmem_limit_bytes=60*2**20))(g, v)

def widen_kernel(g_ref, up_ref, down_ref, out_ref, qkv_ref, stage, sem):
    t = pl.program_id(0)
    slot = lax.rem(t, 2)
    def cols(j): return pl.ds(pl.multiple_of(j * 768, 768), 768)
    def send(ref, s): return pltpu.make_async_copy(stage.at[s], ref, sem.at[s])
    @pl.when(t >= 2)
    def _(): send(out_ref.at[0], slot).wait()
    for b in range(6):
        stage[slot, :, b * 128:(b + 1) * 128] = g_ref[b].astype(F32)
    @pl.when(t < 4)
    def _(): send(up_ref.at[0, :, cols(t)], slot).start()
    @pl.when((t >= 4) & (t < 8))
    def _(): send(down_ref.at[0, cols(t - 4), :], slot).start()
    @pl.when(t == 8)
    def _(): send(out_ref.at[0], slot).start()
    @pl.when(t > 8)
    def _(): send(qkv_ref.at[0, :, cols(t - 9)], slot).start()
    @pl.when(t == 11)
    def _():
        send(out_ref.at[0], 0).wait()
        send(out_ref.at[0], 1).wait()

def widen(g):
    S = jax.ShapeDtypeStruct
    any_ = pl.BlockSpec(memory_space=pl.ANY)
    return pl.pallas_call(widen_kernel, grid=(12,),
        out_shape=(S((1, D, FF), F32), S((1, FF, D), F32), S((1, D, D), F32), S((1, D, 3 * D), F32)),
        in_specs=[pl.BlockSpec((6, 768, 128), lambda t: (t, 0, 0))], out_specs=(any_,) * 4,
        scratch_shapes=[pltpu.VMEM((2, 768, 768), F32), pltpu.SemaphoreType.DMA((2,))],
        compiler_params=pltpu.CompilerParams(vmem_limit_bytes=40 * 2**20))(g)


def body(hidden, text_counts, region_counts, qkv_weight, qv_bias, out_weight, out_bias, norm1_gain, norm1_bias,
         up_weight, up_bias, down_weight, down_bias, norm2_gain, norm2_bias, out_grad):
    mod = lax.axis_index("mod")
    swap = functools.partial(lax.ppermute, axis_name="mod", perm=[(0, 1), (1, 0)])
    h, og = hidden[:, 0], out_grad[:, 0]
    rh = swap(lax.dynamic_slice_in_dim(h, 3 * (1 - mod), 4))
    rog = swap(lax.dynamic_slice_in_dim(og, 4 * (1 - mod), 3))
    y, yo, ig, igo, mid, grads, vec = compute(99, h, rh, og, rog, text_counts, region_counts, qkv_weight[0], qv_bias,
        out_weight[0], out_bias, norm1_gain, norm1_bias, up_weight[0], up_bias, down_weight[0], down_bias, norm2_gain, norm2_bias)
    ry, rig = swap(yo), swap(igo)
    y = lax.dynamic_update_slice_in_dim(y, ry, 4 * (1 - mod), 0)
    ig = lax.dynamic_update_slice_in_dim(ig, rig, 3 * (1 - mod), 0)
    both = mid + lax.dynamic_index_in_dim(rig, 3 * mod, keepdims=False).astype(F32)
    ig = lax.dynamic_update_slice_in_dim(ig, both.astype(BF)[None], 3, 0)
    grads, vec = all_reduce(grads, vec)
    up, down, out, qkv = widen(grads)
    def part(name, n): return vec[:, VEC[name]:VEC[name] + n]
    return (y[:, None], ig[:, None], qkv, part("q", 1536), out, part("out", 768), part("g1", 768), part("b1", 768), up, part("up", 3072),
            down, part("down", 768), part("g2", 768), part("b2", 768))


def solution(mesh):
    rows, pairs, whole = P("batch", "mod", None, None), P("batch"), P()
    return jax.shard_map(body, mesh=mesh, in_specs=(rows, pairs, pairs) + (whole,) * 12 + (rows,),
                         out_specs=(rows, rows) + (whole,) * 12, check_vma=False)
```

time: 607 us -> 286 us (0.47)
  local copies, waits for them, and re-layouts: 191 us -> 13.4 us
  matrix products: 135 us -> 0 us
  Pallas kernels: 103 us -> 235 us
  blocking collectives: 64.6 us -> 0 us
  other arithmetic: 64.9 us -> 0.71 us
  waiting for transfers between devices: 34.6 us -> 28.2 us
    dot_general x18 -> x0, matrix products: 135 us -> none  [the longest x4 32.5 us: row_product(): lax.dot_general(left, right, (((1,), (1,)), ((), ())), preferred_element_...]
    pallas_call x1 -> x3, Pallas kernels: 103 us -> 235 us  [the longest x1 120 us: all_reduce(): pl.pallas_call(functools.partial(ar_kernel, S), out_shape=(jax.ShapeDtype...]
    psum x1 -> x0, blocking collectives: 64.6 us -> none  [body(): summed = lax.psum(tuple((stacked[i] for i in small)), ('mod', 'batch'))]
    convert_element_type x9 -> x0, local copies, waits for them, and re-layouts: 58.7 us -> none  [the longest x5 41.9 us: unblock(): return cut.reshape(1, rows, columns).astype(jnp.float32)]
    reshape x14 -> x0, local copies, waits for them, and re-layouts: 51 us -> none  [the longest x4 24.6 us: blocks(): matrix.astype(jnp.bfloat16)]
    unnamed x104 -> x10, local copies, waits for them, and re-layouts: 44.9 us -> 6.1 us
    convert_element_type x6 -> x0, other arithmetic: 17.5 us -> none  [the longest x2 8.55 us: unblock(): return cut.reshape(1, rows, columns).astype(jnp.float32)]
    reduce_sum x10 -> x0, other arithmetic: 13 us -> none  [the longest x1 4.05 us: body(): jnp.sum(jnp.exp(scores - highest), -1, keepdims=True)]
  transfers between devices with their start and end apart: 4 -> 4, of which waited for: 2 -> 1; matrix products, arithmetic and copies ran while one was open for 19% -> 2% of each run, Pallas kernels for 0% -> 46%
where the time goes in v2:
time: 286 us; the launch traced here: 285 us
  Pallas kernels  235 us (82%)
  waiting for transfers between devices  28.2 us (10%)
  local copies, waits for them, and re-layouts  13.4 us (5%)
  starting transfers between devices  7.05 us (2%)
    pallas_call x1, Pallas kernels, all_reduce(): pl.pallas_call(functools.partial(ar_kernel, S), out_shape=(jax.ShapeDtype...  120 us
    pallas_call x1, Pallas kernels, compute(): pl.pallas_call(functools.partial(compute_kernel, stop), out_shape=(S((7,...  105 us
    ppermute x1, waiting for transfers between devices, body(): rog = swap(lax.dynamic_slice_in_dim(og, 4 * (1 - mod), 3))  28.2 us
    pallas_call x1, Pallas kernels, widen(): pl.pallas_call(widen_kernel, grid=(12,), out_shape=(S((1, D, FF), F32), S...  10.2 us
    unnamed x10, local copies, waits for them, and re-layouts  6.1 us
  transfers between devices with their start and end apart: 4, of which 1 were waited for; matrix products, arithmetic and copies ran while one was open for 2% of the time, Pallas kernels for 46%

profile of v2, /device:TPU:1, one launch (start us, length us, event | category | flops | bytes accessed | tf_op | source)
XLA Modules:
  0.0 285.2 jit_solution(8153814433057940389)
XLA Ops:
  0.6 1.2 dynamic-slice_bitcast_fusion
  1.8 3.7 %collective-permute-start = (bf16[4,128,768]{2,1,0:T(8,128)(2,1)S(1)}, bf16[4,128,768]{2,1,0:T(8,128)(2,1)S(1)}, u32[]{:S(2)}, u32[]{:S(2)}) collective-permute-start(bf16[4,128,768]{2,1,0:T(8,128)(2,1)S(1)} %dynamic-slice_bitcast_fusion), channel_id=1, source_target_pairs={{0,64},{64,0},{1,65},{65,1},{2,66},{66,2},{3,67},{67,3},{4,68},{68... | collective-permute-start | bytes 2359304 | tf_op jit(solution)/shard_map/ppermute | solution.py:517
  5.5 1.1 dynamic-slice_bitcast_fusion.1
  6.6 0.1 collective-permute-start.1
  6.7 28.2 %collective-permute-done.1.rog = bf16[3,128,768]{2,1,0:T(8,128)(2,1)S(1)} collective-permute-done((bf16[3,128,768]{2,1,0:T(8,128)(2,1)S(1)}, bf16[3,128,768]{2,1,0:T(8,128)(2,1)S(1)}, u32[]{:S(2)}, u32[]{:S(2)}) %collective-permute-start.1) | collective-permute-done | bytes 589856 | tf_op jit(solution)/shard_map/ppermute | solution.py:518
  34.9 0.0 copy-start.2
  34.9 0.0 collective-permute-done.rhid
  34.9 0.0 copy-start.1
  34.9 0.8 copy-done.2
  35.7 0.3 copy-done.1
  36.0 104.7 %shard_map.263 = (bf16[7,128,768]{2,1,0:T(8,128)(2,1)}, bf16[3,128,768]{2,1,0:T(8,128)(2,1)}, bf16[7,128,768]{2,1,0:T(8,128)(2,1)}, bf16[4,128,768]{2,1,0:T(8,12...) custom-call(bf16[7,128,768]{2,1,0:T(8,128)(2,1)} %bitcast.30, ...), custom_call_target="tpu_custom_call" | custom-call | tf_op jit(solution)/shard_map/pallas_call | solution.py:314
  140.7 3.2 %collective-permute-start.2 = (bf16[3,128,768]{2,1,0:T(8,128)(2,1)}, bf16[3,128,768]{2,1,0:T(8,128)(2,1)S(1)}, u32[]{:S(2)}, u32[]{:S(2)}) collective-permute-start(bf16[3,128,768]{2,1,0:T(8,128)(2,1)} %get-tuple-element.28), channel_id=1, source_target_pairs={{0,64},{64,0},{1,65},{65,1},{2,66},{66,2},{3,67},{67,3},{4,68},{68... | collective-permute-start | bytes 1769480 | tf_op jit(solution)/shard_map/ppermute | solution.py:521
  143.9 0.1 collective-permute-start.3
  144.0 120.3 %shard_map.264 = (bf16[72,768,128]{2,1,0:T(8,128)(2,1)}, f32[1,9216]{1,0:T(1,128)}) custom-call(bf16[72,768,128]{2,1,0:T(8,128)(2,1)} %get-tuple-element.32.g_ref, f32[1,9216]{1,0:T(1,128)} %get-tuple-element.33.v_ref), custom_call_target="tpu_custom_call" | custom-call | tf_op jit(solution)/shard_map/pallas_call | solution.py:473
  264.3 1.3 slice.24
  265.6 1.3 slice.28
  266.9 0.0 copy-start
  266.9 5.0 %copy-done = bf16[72,768,128]{2,1,0:T(8,128)(2,1)S(1)} copy-done((bf16[72,768,128]{2,1,0:T(8,128)(2,1)S(1)}, bf16[72,768,128]{2,1,0:T(8,128)(2,1)}, u32[]{:S(2)}) %copy-start) | copy-done | bytes 14155800
  271.9 0.0 copy-start.4
  271.9 10.2 %shard_map.265 = (f32[1,768,3072]{2,1,0:T(8,128)}, f32[1,3072,768]{2,1,0:T(8,128)}, f32[1,768,768]{2,1,0:T(8,128)}, f32[1,768,2304]{2,1,0:T(8,128)}) custom-call(bf16[72,768,128]{2,1,0:T(8,128)(2,1)S(1)} %copy-done), custom_call_target="tpu_custom_call" | custom-call | tf_op jit(solution)/shard_map/pallas_call | solution.py:505
  282.1 0.0 copy-done.4
  282.1 0.6 fusion.3
  282.7 0.0 collective-permute-done.2
  282.7 0.0 copy-start.3
  282.7 0.9 bitcast_dynamic-update-slice_fusion.1
  283.6 0.0 collective-permute-done.3
  283.6 0.9 bitcast_dynamic-update-slice_fusion
  284.5 0.0 copy-done.3
  284.5 0.7 fusion.2
Async XLA Ops:
  1.8 33.1 %collective-permute-start = (bf16[4,128,768]{2,1,0:T(8,128)(2,1)S(1)}, bf16[4,128,768]{2,1,0:T(8,128)(2,1)S(1)}, u32[]{:S(2)}, u32[]{:S(2)}) collective-permute-start(bf16[4,128,768]{2,1,0:T(8,128)(2,1)S(1)} %dynamic-slice_bitcast_fusion), channel_id=1, source_target_pairs={{0,64},{64,0},{1,65},{65,1},{2,66},{66,2},{3,67},{67,3},{4,68},{68... | collective-permute-start | bytes 2359304 | tf_op jit(solution)/shard_map/ppermute | solution.py:517
  6.6 28.3 %collective-permute-start.1 = (bf16[3,128,768]{2,1,0:T(8,128)(2,1)S(1)}, bf16[3,128,768]{2,1,0:T(8,128)(2,1)S(1)}, u32[]{:S(2)}, u32[]{:S(2)}) collective-permute-start(bf16[3,128,768]{2,1,0:T(8,128)(2,1)S(1)} %dynamic-slice_bitcast_fusion.1), channel_id=1, source_target_pairs={{0,64},{64,0},{1,65},{65,1},{2,66},{66,2},{3,67},{67,3},{4,68},{68... | collective-permute-start | bytes 1769480 | tf_op jit(solution)/shard_map/ppermute | solution.py:518
  34.9 0.8 copy-start.2
  34.9 1.1 copy-start.1
  140.7 142.0 %collective-permute-start.2 = (bf16[3,128,768]{2,1,0:T(8,128)(2,1)}, bf16[3,128,768]{2,1,0:T(8,128)(2,1)S(1)}, u32[]{:S(2)}, u32[]{:S(2)}) collective-permute-start(bf16[3,128,768]{2,1,0:T(8,128)(2,1)} %get-tuple-element.28), channel_id=1, source_target_pairs={{0,64},{64,0},{1,65},{65,1},{2,66},{66,2},{3,67},{67,3},{4,68},{68... | collective-permute-start | bytes 1769480 | tf_op jit(solution)/shard_map/ppermute | solution.py:521
  143.9 139.6 %collective-permute-start.3 = (bf16[4,128,768]{2,1,0:T(8,128)(2,1)}, bf16[4,128,768]{2,1,0:T(8,128)(2,1)S(1)}, u32[]{:S(2)}, u32[]{:S(2)}) collective-permute-start(bf16[4,128,768]{2,1,0:T(8,128)(2,1)} %get-tuple-element.30), channel_id=1, source_target_pairs={{0,64},{64,0},{1,65},{65,1},{2,66},{66,2},{3,67},{67,3},{4,68},{68... | collective-permute-start | bytes 2359304 | tf_op jit(solution)/shard_map/ppermute | solution.py:521
  266.9 5.0 %copy-start = (bf16[72,768,128]{2,1,0:T(8,128)(2,1)S(1)}, bf16[72,768,128]{2,1,0:T(8,128)(2,1)}, u32[]{:S(2)}) copy-start(bf16[72,768,128]{2,1,0:T(8,128)(2,1)} %get-tuple-element.34.g_ref) | copy-start | bytes 42467332
  271.9 10.2 %copy-start.4 = (f32[1,9216]{1,0:T(1,128)S(1)}, f32[1,9216]{1,0:T(1,128)}, u32[]{:S(2)}) copy-start(f32[1,9216]{1,0:T(1,128)} %get-tuple-element.36) | copy-start | bytes 110596
  282.7 1.8 copy-start.3
